TPU v7x, 32 devices: a whole 2x2x4 slice. The times are simulated.
32 devices in a mesh: grp: 4 (over y, x), vid: 8 (over z, core).
Axes of the slice: x: 2, y: 2, z: 4, core: 2. Of those that a mesh axis runs over, the one named last changes fastest.
Arguments:
- frames: bfloat16 [32768, 1024], P(('grp', 'vid')), parts along dimension 0, may hold values from -240 to 240
- w_frame: bfloat16 [1024, 512], replicated, may hold values from -0.1875 to 0.1875
- step_emb: bfloat16 [4096, 512], P(('grp', 'vid')), parts along dimension 0, may hold values from -6 to 6
- targets: int32 [32768], P(('grp', 'vid')), parts along dimension 0, may hold values from 0 to 127
- tile_frame: int32 [32, 64], P(('grp', 'vid')), parts along dimension 0, may hold values from 0 to 7, as said below
- tile_step: int32 [32, 64], P(('grp', 'vid')), parts along dimension 0, may hold values from 0 to 7, as said below
- tile_count: int32 [32], P(('grp', 'vid')), parts along dimension 0, may hold values from 8 to 64, as said below
Outputs:
- row_loss: float32 [32768], P(('grp', 'vid')), parts along dimension 0
- frame_grad: bfloat16 [32768, 1024], P(('grp', 'vid')), parts along dimension 0
- step_grad: float32 [4096, 512], P(('grp', 'vid')), parts along dimension 0
There are 4 independent parts, one for each index of `grp`. A program takes and returns all parts, laid end to end along the dimension named above; an argument that names none is the same for every part. Nothing has to cross between parts.
Inputs may be any that keep to these rules, and one draw needn't show every extreme that they name: `tile_frame`: each run of 8 tiles of a list, starting at a multiple of 8, names every frame block once. `tile_step`: the (frame block, step block) pairs of one video's list are distinct; the first 8 tiles pair each frame block with the video's own step block. Only the first tile_count tiles of a list are valid; some video's list is full.
All inputs are finite; a program needn't handle non-finite values.
Results may differ from a plain program's by a relative error of at most 0.0086.
Values may be sent and summed in bfloat16 or wider, within the bound.
No kernel may reach another device: no remote copies, remote signals or barrier semaphores. Data moves between devices by JAX's collectives and lax.ppermute only.
A program may use at most 128 MiB of HBM per device.

v0:
```python
import math

import jax
import jax.numpy as jnp
from jax import lax
from jax.experimental import pallas as pl
from jax.experimental.pallas import tpu as pltpu
from jax.sharding import PartitionSpec as P

F32 = jnp.float32
BF16 = jnp.bfloat16
HIDDEN = -1e30
EMBED_MIB = 52
TILES = 4
PIECES = 4
WIDE = 256
NT = (((1,), (1,)), ((), ()))
TN = (((0,), (0,)), ((), ()))
VMEM = pl.BlockSpec(memory_space=pltpu.VMEM)
SMEM = pl.BlockSpec(memory_space=pltpu.SMEM)
ANYWHERE = pl.BlockSpec(memory_space=pl.ANY)


def params(mib):
    return pltpu.CompilerParams(vmem_limit_bytes=mib * 2**20)


def cost(flops, nbytes, exps=0):
    return pl.CostEstimate(flops=flops, bytes_accessed=nbytes, transcendentals=exps)


def embed_kernel(x_hbm, w_hbm, e_ref, x_ref, w_ref, sem):
    tile = x_ref.shape[0] // TILES
    deep = w_ref.shape[0] // TILES
    reads = []
    for n in range(TILES):
        at = pl.ds(n * deep, deep)
        reads.append(pltpu.make_async_copy(w_hbm.at[at], w_ref.at[at], sem.at[n]))
    for n in range(TILES):
        at = pl.ds(n * tile, tile)
        reads.append(pltpu.make_async_copy(x_hbm.at[at], x_ref.at[at], sem.at[TILES + n]))
    for read in reads:
        read.start()
    for read in reads[:TILES]:
        read.wait()
    for n in range(TILES):
        reads[TILES + n].wait()
        at = slice(n * tile, (n + 1) * tile)
        e_ref[at, :] = jnp.dot(x_ref[at, :], w_ref[...], preferred_element_type=F32).astype(BF16)


def embed(frames, w):
    rows, depth = frames.shape
    width = w.shape[1]
    return pl.pallas_call(
        embed_kernel,
        in_specs=[ANYWHERE, ANYWHERE],
        out_specs=VMEM,
        out_shape=jax.ShapeDtypeStruct((rows, width), BF16),
        scratch_shapes=[
            pltpu.VMEM((rows, depth), BF16),
            pltpu.VMEM((depth, width), BF16),
            pltpu.SemaphoreType.DMA((2 * TILES,)),
        ],
        cost_estimate=cost(2 * rows * depth * width, 2 * (rows * depth + depth * width + rows * width)),
        compiler_params=params(EMBED_MIB),
        name="embed",
    )(frames, w)


def sight_kernel(place_ref, count_ref, tf_ref, ts_ref, keep_ref, give_ref):
    chips, rows = keep_ref.shape
    slots = tf_ref.shape[1]
    line = lax.broadcasted_iota(jnp.int32, (chips, slots), 0)
    slot = lax.broadcasted_iota(jnp.int32, (chips, slots), 1)
    block = lax.broadcasted_iota(jnp.int32, (rows, slots), 0) // 128
    right = jnp.where(tf_ref[...] == block, 1.0, 0.0).astype(BF16)
    for core, out_ref in enumerate((keep_ref, give_ref)):
        video = (2 * line + core) ^ place_ref[0]
        left = jnp.where((ts_ref[...] == video) & (slot < count_ref[0]), 1.0, 0.0).astype(BF16)
        seen = lax.dot_general(left, right, NT, preferred_element_type=F32)
        out_ref[...] = jnp.where(seen > 0.5, 0.0, HIDDEN)


def sight(place, count, tf, ts, chips, rows):
    return pl.pallas_call(
        sight_kernel,
        in_specs=[SMEM, SMEM, VMEM, VMEM],
        out_specs=[VMEM, VMEM],
        out_shape=[jax.ShapeDtypeStruct((chips, rows), F32)] * 2,
        compiler_params=params(24),
        name="sight",
    )(place, count, tf, ts)


def columns(rows):
    for half in range(2):
        for at in range(0, rows, WIDE):
            yield half, slice(at, at + WIDE), slice(half * rows + at, half * rows + at + WIDE)


def score_kernel(ks, temper, *refs):
    n = len(ks)
    es, biases = refs[:2], refs[2:4]
    blocks = refs[4 : 4 + n]
    refs = refs[4 + n :]
    if 0 in ks:
        goal_ref, st_in = refs[0], None
    else:
        st_in = refs[0]
    ps, top_ref, st_ref = refs[1 : 1 + n], refs[1 + n], refs[2 + n]
    rows, own = es[0].shape[0], blocks[0].shape[0]
    table = blocks[0][...] if n == 1 else jnp.concatenate([ref[...] for ref in blocks], axis=0)
    for half, at, to in columns(rows):
        s = lax.dot_general(table, es[half][at, :], NT, preferred_element_type=F32) * temper
        cuts = [s[m * own : (m + 1) * own] for m in range(n)]
        if 0 in ks and half == 0:
            hit = goal_ref[:, at] == lax.broadcasted_iota(jnp.int32, (own, WIDE), 0)
            found = jnp.sum(jnp.where(hit, cuts[ks.index(0)], 0.0), axis=0, keepdims=True)
            refs[3 + n][:, at] = found
        top = None if st_in is None else st_in[0:1, to]
        for m, k in enumerate(ks):
            cuts[m] = cuts[m] + biases[half][k : k + 1, at]
            high = jnp.max(cuts[m], axis=0, keepdims=True)
            top = high if top is None else jnp.maximum(top, high)
        total = None if st_in is None else st_in[1:2, to] * jnp.exp(st_in[0:1, to] - top)
        for m in range(n):
            p = jnp.exp(cuts[m] - top)
            ps[m][:, to] = p
            part = jnp.sum(p, axis=0, keepdims=True)
            total = part if total is None else total + part
        top_ref[:, to] = top
        st_ref[0:1, to] = top
        st_ref[1:2, to] = total


def score(ks, temper, es, biases, blocks, last):
    rows, width = es[0].shape
    own = blocks[0].shape[0]
    shapes = [jax.ShapeDtypeStruct((own, 2 * rows), F32)] * len(ks)
    shapes += [jax.ShapeDtypeStruct((1, 2 * rows), F32)]
    shapes += [jax.ShapeDtypeStruct((2, 2 * rows), F32)]
    shapes += [jax.ShapeDtypeStruct((1, rows), F32)] * (0 in ks)
    made = pl.pallas_call(
        lambda *refs: score_kernel(ks, temper, *refs),
        in_specs=[VMEM] * (5 + len(ks)),
        out_specs=[VMEM] * len(shapes),
        out_shape=shapes,
        cost_estimate=cost(
            4 * len(ks) * own * rows * width, 4 * rows * width + 8 * len(ks) * own * rows
        ),
        compiler_params=params(24),
        name=f"score_{ks[-1]}",
    )(*es, *biases, *blocks, last)
    return made[: len(ks)], made[len(ks)], made[len(ks) + 1 :]


def share_kernel(ks, *refs):
    st_ref, got_ref = refs[:2]
    es = refs[2:4]
    n = len(ks)
    ps, tops = refs[4 : 4 + n], refs[4 + n : 4 + 2 * n]
    refs = refs[4 + 2 * n :]
    if 0 in ks:
        goal_ref, pos_ref = refs[:2]
        refs = refs[2:]
    qs, outs = refs[:n], refs[n : 2 * n]
    rows = es[0].shape[0]
    for half in range(2):
        here = slice(half * rows, (half + 1) * rows)
        there = slice((1 - half) * rows, (2 - half) * rows)
        top, other = st_ref[0:1, here], got_ref[0:1, there]
        last = jnp.maximum(top, other)
        total = st_ref[1:2, here] * jnp.exp(top - last) + got_ref[1:2, there] * jnp.exp(other - last)
        if 0 in ks and half == 0:
            refs[2 * n][...] = last + jnp.log(total) - pos_ref[...]
        inverse = 1.0 / total
        for m, k in enumerate(ks):
            scale = jnp.exp(tops[m][:, here] - last) * inverse
            for at in range(0, rows, WIDE):
                to = slice(half * rows + at, half * rows + at + WIDE)
                q = (ps[m][:, to] * scale[:, at : at + WIDE]).astype(BF16)
                if k == 0 and half == 0:
                    hit = goal_ref[:, to] == lax.broadcasted_iota(jnp.int32, q.shape, 0)
                    q = (q.astype(F32) - jnp.where(hit, 1.0, 0.0)).astype(BF16)
                qs[m][:, to] = q
    for m in range(n):
        out = jnp.dot(qs[m][:, :rows], es[0][...], preferred_element_type=F32)
        out = out + jnp.dot(qs[m][:, rows:], es[1][...], preferred_element_type=F32)
        outs[m][...] = out.astype(outs[m].dtype)


def share(ks, kept, st, got, es, *more):
    own, rows2 = kept[ks[0]][0].shape
    width = es[0].shape[1]
    n = len(ks)
    shapes = [jax.ShapeDtypeStruct((own, rows2), BF16)] * n
    shapes += [jax.ShapeDtypeStruct((own, width), BF16 if k % 2 else F32) for k in ks]
    shapes += [jax.ShapeDtypeStruct((1, rows2 // 2), F32)] * (0 in ks)
    made = pl.pallas_call(
        lambda *refs: share_kernel(ks, *refs),
        in_specs=[VMEM] * (4 + 2 * n + len(more)),
        out_specs=[VMEM] * len(shapes),
        out_shape=shapes,
        cost_estimate=cost(2 * n * own * rows2 * width, n * 6 * own * rows2 + 2 * rows2 * width),
        compiler_params=params(40),
        name=f"share_{ks[0]}",
    )(st, got, *es, *[kept[k][0] for k in ks], *[kept[k][1] for k in ks], *more)
    return made[:n], made[n : 2 * n], made[2 * n :]


def part_rows(qs, table, at):
    q = jnp.concatenate([q_ref[:, at] for q_ref in qs], axis=0)
    return lax.dot_general(q, table, TN, preferred_element_type=F32)


def rows_kernel(n, first, *refs):
    table = jnp.concatenate([ref[...] for ref in refs[n : 2 * n]], axis=0)
    for turn, out_ref in enumerate(refs[2 * n :]):
        base = first + turn * out_ref.shape[0]
        for at in range(0, out_ref.shape[0], WIDE):
            part = part_rows(refs[:n], table, slice(base + at, base + at + WIDE))
            out_ref[at : at + WIDE, :] = part.astype(out_ref.dtype)


def rows_of(qs, blocks, theirs):
    n = len(qs)
    own, rows2 = qs[0].shape
    rows, width = rows2 // 2, blocks[0].shape[1]
    cut = PIECES if theirs else 1
    shape = jax.ShapeDtypeStruct((rows // cut, width), BF16 if theirs else F32)
    return pl.pallas_call(
        lambda *refs: rows_kernel(n, rows if theirs else 0, *refs),
        in_specs=[VMEM] * (2 * n),
        out_specs=[VMEM] * cut,
        out_shape=[shape] * cut,
        cost_estimate=cost(n * own * rows2 * width, 2 * n * own * (rows2 + width)),
        compiler_params=params(24),
        name="rows_theirs" if theirs else "rows_mine",
    )(*qs, *blocks)


def back_kernel(temper, mine_ref, w_ref, *refs):
    *gots, out_hbm, out_ref, sem = refs
    size = gots[0].shape[0]
    writes = []
    for turn, at in enumerate(range(0, out_ref.shape[0], WIDE)):
        cut = slice(at, at + WIDE)
        inner = slice(at % size, at % size + WIDE)
        g = (mine_ref[cut, :] + gots[at // size][inner, :].astype(F32)) * temper
        out_ref[cut, :] = lax.dot_general(
            g.astype(BF16), w_ref[...], NT, preferred_element_type=F32
        ).astype(BF16)
        cut = pl.ds(at, WIDE)
        writes.append(pltpu.make_async_copy(out_ref.at[cut], out_hbm.at[cut], sem.at[turn]))
        writes[-1].start()
    for write in writes:
        write.wait()


def back(mine, gots, w, temper):
    rows, width = mine.shape
    depth = w.shape[0]
    return pl.pallas_call(
        lambda *refs: back_kernel(temper, *refs),
        in_specs=[VMEM] * (2 + len(gots)),
        out_specs=ANYWHERE,
        out_shape=jax.ShapeDtypeStruct((rows, depth), BF16),
        scratch_shapes=[
            pltpu.VMEM((rows, depth), BF16),
            pltpu.SemaphoreType.DMA((rows // WIDE,)),
        ],
        cost_estimate=cost(2 * rows * width * depth, 2 * (depth * width + rows * depth)),
        compiler_params=params(40),
        name="back",
    )(mine, w, *gots)


def shards(frames, w_frame, step_emb, targets, tile_frame, tile_step, tile_count):
    videos = lax.axis_size("vid")
    chips = videos // 2
    rows = frames.shape[0]
    temper = 1.0 / math.sqrt(step_emb.shape[1])
    place = lax.axis_index("vid").astype(jnp.int32).reshape(1)
    goals = targets.reshape(1, -1)

    def trade(x, k):
        return lax.ppermute(x, "vid", [(i, i ^ k) for i in range(videos)])

    order, bit = [0], chips // 2
    while bit:
        order += [k ^ bit for k in order]
        bit //= 2
    e = embed(frames, w_frame)
    keep, lend = sight(place, tile_count, tile_frame, tile_step, chips, rows)
    biases = (keep, trade(lend, 1))
    mine, kept, st = {0: step_emb}, {}, goals
    near = trade(step_emb, 2)
    far = chips // 2
    come = trade(step_emb, 2 * far)
    mine[1], mine[far], e = lax.optimization_barrier((near, come, e))
    es = (e, trade(e, 1))
    early = (0, far, 1)
    for ks in [early] + [(k,) for k in order if k not in early]:
        k = ks[0]
        if k > 0:
            low = k & -k
            come = trade(mine[k ^ low], 2 * low)
            mine[k], gate = lax.optimization_barrier((come, st))
        ps, top, (st, *pos) = score(ks, temper, es, biases, [mine[m] for m in ks], st)
        if pos:
            found = pos[0]
        for m, p in zip(ks, ps):
            kept[m] = (p, top)
    got = trade(st, 1)

    qs, sums = {}, {}
    for ks in [(k,) for k in range(chips - 1, 2, -1)] + [(2, 1, 0)]:
        more = (goals, found) if 0 in ks else ()
        made, parts, loss = share(ks, kept, st, got, es, *more)
        qs.update(zip(ks, made))
        sums.update(zip(ks, parts))
        if 0 not in ks:
            e, qs[ks[0]] = lax.optimization_barrier((es[0], qs[ks[0]]))
            es = (e, es[1])
    parts = [qs[k] for k in order], [mine[k] for k in order]
    lent = [trade(piece, 1) for piece in rows_of(*parts, True)]
    (own_rows,) = rows_of(*parts, False)
    frame_grad = back(own_rows, lent, w_frame, temper)
    bit = 1
    while bit < chips:
        for k in range(chips - bit, 0, -2 * bit):
            come = trade(sums[k].astype(BF16), 2 * bit)
            if 2 * bit == chips:
                come, frame_grad = lax.optimization_barrier((come, frame_grad))
            sums[k - bit] = sums[k - bit].astype(F32) + come.astype(F32)
        bit *= 2
    return (loss[0].reshape(-1), frame_grad, sums[0] * temper)


def solution(mesh):
    placed = (
        P(("grp", "vid"), None),
        P(),
        P(("grp", "vid"), None),
        P(("grp", "vid")),
        P(("grp", "vid"), None),
        P(("grp", "vid"), None),
        P(("grp", "vid")),
    )
    return jax.shard_map(
        shards,
        mesh=mesh,
        in_specs=placed,
        out_specs=(P(("grp", "vid")), P(("grp", "vid"), None), P(("grp", "vid"), None)),
        check_vma=False,
    )
```

profile of v0, /device:TPU:0, one launch (start us, length us, event | category | flops | bytes accessed | tf_op | source)
XLA Modules:
  0.0 36.2 jit_solution(5982413444690992674)
XLA Ops:
  0.7 4.1 %collective-permute-start.1 = (bf16[128,512]{1,0:T(8,128)(2,1)}, bf16[128,512]{1,0:T(8,128)(2,1)S(1)}, u32[]{:S(2)}, u32[]{:S(2)}) collective-permute-start(bf16[128,512]{1,0:T(8,128)(2,1)} %refs_4_.5), channel_id=1, source_target_pairs={{0,4},{1,5},{2,6},{3,7},{4,0},{5,1},{6,2},{7,3},{8,12},{9,13},{10,... | collective-permute-start | bytes 393224 | tf_op jit(solution)/shard_map/ppermute | solution.py:288
  4.8 1.6 %collective-permute-start = (bf16[128,512]{1,0:T(8,128)(2,1)}, bf16[128,512]{1,0:T(8,128)(2,1)S(1)}, u32[]{:S(2)}, u32[]{:S(2)}) collective-permute-start(bf16[128,512]{1,0:T(8,128)(2,1)} %refs_4_.5), channel_id=1, source_target_pairs={{0,2},{1,3},{2,0},{3,1},{4,6},{5,7},{6,4},{7,5},{8,10},{9,11},{10,... | collective-permute-start | bytes 393224 | tf_op jit(solution)/shard_map/ppermute | solution.py:288
  6.3 3.2 %embed.1.refs_0_.refs_2_ = bf16[1024,512]{1,0:T(8,128)(2,1)S(1)} custom-call(bf16[1024,1024]{1,0:T(8,128)(2,1)} %x_hbm.1, bf16[1024,512]{1,0:T(8,128)(2,1)} %refs_1_.1), custom_call_target="tpu_custom_call" | custom-call | flops 1073741824 | bytes 4194304 | tf_op jit(solution)/shard_map/embed/pallas_call | solution.py:55
  9.5 1.9 %collective-permute-done.1.refs_5_ = bf16[128,512]{1,0:T(8,128)(2,1)S(1)} collective-permute-done((bf16[128,512]{1,0:T(8,128)(2,1)}, bf16[128,512]{1,0:T(8,128)(2,1)S(1)}, u32[]{:S(2)}, u32[]{:S(2)}) %collective-permute-start.1) | collective-permute-done | bytes 131104 | tf_op jit(solution)/shard_map/ppermute | solution.py:288
  11.4 0.2 collective-permute-done.refs_6_
  11.6 1.4 %collective-permute-start.4 = (bf16[128,512]{1,0:T(8,128)(2,1)S(1)}, bf16[128,512]{1,0:T(8,128)(2,1)S(1)}, u32[]{:S(2)}, u32[]{:S(2)}) collective-permute-start(bf16[128,512]{1,0:T(8,128)(2,1)S(1)} %collective-permute-done.1.refs_5_), channel_id=1, source_target_pairs={{0,2},{1,3},{2,0},{3,1},{4,6},{5,7},{6,4},{7,5},{8,10},{9,11},{10,... | collective-permute-start | bytes 393224 | tf_op jit(solution)/shard_map/ppermute | solution.py:288
  13.7 0.3 sight.1
  14.0 0.3 collective-permute-start.3
  14.3 1.0 %collective-permute-done.3.refs_3_ = f32[4,1024]{1,0:T(4,128)S(1)} collective-permute-done((f32[4,1024]{1,0:T(4,128)S(1)}, f32[4,1024]{1,0:T(4,128)S(1)}, u32[]{:S(2)}, u32[]{:S(2)}) %collective-permute-start.3) | collective-permute-done | bytes 16416 | tf_op jit(solution)/shard_map/ppermute | solution.py:288
  15.2 1.4 %score_1.1 = (f32[128,2048]{1,0:T(8,128)S(1)}, f32[128,2048]{1,0:T(8,128)S(1)}, f32[128,2048]{1,0:T(8,128)S(1)}, f32[1,2048]{1,0:T(1,128)S(1)}, f32[2,2048]{1,0:T(2,128)S(1)}, /*index=5*/f32[1,1024]{1,0:T(1,128)S(1)}) custom-call(bf16[1024,512]{1,0:T(8,128)(2,1)S(1)} %embed.1.refs_0_.refs_2_, bf16[1024,512]{1,0:T(8,128)(2,1)S(1)} %collective-permute-done.2.refs_1_.refs_3_, ...), custom_call_target="tpu_custom_call" | custom-call | flops 805306368 | bytes 5242880 | tf_op jit(solution)/shard_map/score_1/pallas_call | solution.py:144
  16.6 0.9 %collective-permute-done.4.refs_4_.refs_7_ = bf16[128,512]{1,0:T(8,128)(2,1)S(1)} collective-permute-done((bf16[128,512]{1,0:T(8,128)(2,1)S(1)}, bf16[128,512]{1,0:T(8,128)(2,1)S(1)}, u32[]{:S(2)}, u32[]{:S(2)}) %collective-permute-start.4) | collective-permute-done | bytes 131104 | tf_op jit(solution)/shard_map/ppermute | solution.py:288
  17.5 0.9 %score_3.1 = (f32[128,2048]{1,0:T(8,128)S(1)}, f32[1,2048]{1,0:T(1,128)S(1)}, f32[2,2048]{1,0:T(2,128)S(1)}) custom-call(bf16[1024,512]{1,0:T(8,128)(2,1)S(1)} %embed.1.refs_0_.refs_2_, bf16[1024,512]{1,0:T(8,128)(2,1)S(1)} %collective-permute-done.2.refs_1_.refs_3_, f32[4,1024]{1,0:T(4,128)S(1)} %get-tuple-element.36.refs_2_, ...), custom_call_target="tpu_custom_call" | custom-call | flops 268435456 | bytes 3145728 | tf_op jit(solution)/shard_map/score_3/pallas_call | solution.py:144
  18.4 0.1 collective-permute-start.5
  18.5 1.2 %collective-permute-done.5.refs_1_ = f32[2,2048]{1,0:T(2,128)S(1)} collective-permute-done((f32[2,2048]{1,0:T(2,128)S(1)}, f32[2,2048]{1,0:T(2,128)S(1)}, u32[]{:S(2)}, u32[]{:S(2)}) %collective-permute-start.5) | collective-permute-done | bytes 16416 | tf_op jit(solution)/shard_map/ppermute | solution.py:288
  19.6 0.4 %share_3.1 = (bf16[128,2048]{1,0:T(8,128)(2,1)S(1)}, bf16[128,512]{1,0:T(8,128)(2,1)S(1)}) custom-call(f32[2,2048]{1,0:T(2,128)S(1)} %get-tuple-element.42.refs_0_, f32[2,2048]{1,0:T(2,128)S(1)} %collective-permute-done.5.refs_1_, bf16[1024,512]{1,0:T(8,128)(2,1)S(1)} %embed.1.refs_0_.refs_2_, bf16[1024,512]{1,0:T(8,128)(2,1)S(1)} %collective-permute-done.2.refs_1_.refs_3_, ...), custom_call_target="tpu_custom_call" | custom-call | flops 268435456 | bytes 3670016 | tf_op jit(solution)/shard_map/share_3/pallas_call | solution.py:200
  20.1 1.5 %collective-permute-start.6 = (bf16[128,512]{1,0:T(8,128)(2,1)S(1)}, bf16[128,512]{1,0:T(8,128)(2,1)S(1)}, u32[]{:S(2)}, u32[]{:S(2)}) collective-permute-start(bf16[128,512]{1,0:T(8,128)(2,1)S(1)} %get-tuple-element.54), channel_id=1, source_target_pairs={{0,2},{1,3},{2,0},{3,1},{4,6},{5,7},{6,4},{7,5},{8,10},{9,11},{10,... | collective-permute-start | bytes 393224 | tf_op jit(solution)/shard_map/ppermute | solution.py:288
  21.6 1.5 %share_2.1 = (bf16[128,2048]{1,0:T(8,128)(2,1)S(1)}, bf16[128,2048]{1,0:T(8,128)(2,1)S(1)}, bf16[128,2048]{1,0:T(8,128)(2,1)S(1)}, f32[128,512]{1,0:T(8,128)S(1)...) custom-call(f32[2,2048]{1,0:T(2,128)S(1)} %get-tuple-element.42.refs_0_, ...), custom_call_target="tpu_custom_call" | custom-call | flops 805306368 | bytes 6815744 | tf_op jit(solution)/shard_map/share_2/pallas_call | solution.py:200
  23.1 0.7 %rows_theirs.1 = (bf16[256,512]{1,0:T(8,128)(2,1)S(1)}, bf16[256,512]{1,0:T(8,128)(2,1)S(1)}, bf16[256,512]{1,0:T(8,128)(2,1)S(1)}, bf16[256,512]{1,0:T(8,128)(2,1)S(1)}) custom-call(bf16[128,2048]{1,0:T(8,128)(2,1)S(1)} %get-tuple-element.55.refs_0_, bf16[128,2048]{1,0:T(8,128)(2,1)S(1)} %get-tuple-element.56.refs_1_, ...), custom_call_target="tpu_custom_call" | custom-call | flops 536870912 | bytes 2621440 | tf_op jit(solution)/shard_map/rows_theirs/pallas_call | solution.py:232
  23.8 0.1 collective-permute-start.8
  23.9 0.6 %collective-permute-start.12 = (bf16[128,512]{1,0:T(8,128)(2,1)S(1)}, bf16[128,512]{1,0:T(8,128)(2,1)S(1)}, u32[]{:S(2)}, u32[]{:S(2)}) collective-permute-start(bf16[128,512]{1,0:T(8,128)(2,1)S(1)} %get-tuple-element.65), channel_id=1, source_target_pairs={{0,2},{1,3},{2,0},{3,1},{4,6},{5,7},{6,4},{7,5},{8,10},{9,11},{10,... | collective-permute-start | bytes 393224 | tf_op jit(solution)/shard_map/ppermute | solution.py:288
  24.5 0.2 collective-permute-start.9
  24.7 0.3 collective-permute-start.10
  25.1 0.7 %collective-permute-done.6 = bf16[128,512]{1,0:T(8,128)(2,1)S(1)} collective-permute-done((bf16[128,512]{1,0:T(8,128)(2,1)S(1)}, bf16[128,512]{1,0:T(8,128)(2,1)S(1)}, u32[]{:S(2)}, u32[]{:S(2)}) %collective-permute-start.6) | collective-permute-done | bytes 131104 | tf_op jit(solution)/shard_map/ppermute | solution.py:288
  25.8 0.0 copy-start
  25.8 0.0 collective-permute-done.8.refs_2_
  25.8 2.1 %collective-permute-start.7 = (bf16[128,512]{1,0:T(8,128)(2,1)S(1)}, bf16[128,512]{1,0:T(8,128)(2,1)S(1)}, u32[]{:S(2)}, u32[]{:S(2)}) collective-permute-start(bf16[128,512]{1,0:T(8,128)(2,1)S(1)} %add_convert_fusion), channel_id=1, source_target_pairs={{0,4},{1,5},{2,6},{3,7},{4,0},{5,1},{6,2},{7,3},{8,12},{9,13},{10,... | collective-permute-start | bytes 393224 | tf_op jit(solution)/shard_map/ppermute | solution.py:288
  27.9 0.7 %rows_mine.1.refs_0_ = f32[1024,512]{1,0:T(8,128)S(1)} custom-call(bf16[128,2048]{1,0:T(8,128)(2,1)S(1)} %get-tuple-element.55.refs_0_, bf16[128,2048]{1,0:T(8,128)(2,1)S(1)} %get-tuple-element.56.refs_1_, bf16[128,2048]{1,0:T(8,128)(2,1)S(1)} %get-tuple-element.57.refs_2_, bf16[128,2048]{1,0:T(8,128)(2,1)S(1)} %get-tuple-element.58.refs_3_, ...), custom_call_target="tpu_custom_call" | custom-call | flops 536870912 | bytes 2621440 | tf_op jit(solution)/shard_map/rows_mine/pallas_call | solution.py:232
  28.7 0.0 collective-permute-done.9.refs_3_
  28.7 0.0 collective-permute-done.10.refs_4_
  28.7 2.1 %back.1 = bf16[1024,1024]{1,0:T(8,128)(2,1)} custom-call(f32[1024,512]{1,0:T(8,128)S(1)} %rows_mine.1.refs_0_, bf16[1024,512]{1,0:T(8,128)(2,1)S(1)} %copy-done, bf16[256,512]{1,0:T(8,128)(2,1)S(1)} %collective-permute-done.8.refs_2_, bf16[256,512]{1,0:T(8,128)(2,1)S(1)} %collective-permute-done.9.refs_3_, ...), custom_call_target="tpu_custom_call" | custom-call | flops 1073741824 | bytes 3145728 | tf_op jit(solution)/shard_map/back/pallas_call | solution.py:264
  30.9 4.6 %collective-permute-done.7 = bf16[128,512]{1,0:T(8,128)(2,1)S(1)} collective-permute-done((bf16[128,512]{1,0:T(8,128)(2,1)S(1)}, bf16[128,512]{1,0:T(8,128)(2,1)S(1)}, u32[]{:S(2)}, u32[]{:S(2)}) %collective-permute-start.7) | collective-permute-done | bytes 131104 | tf_op jit(solution)/shard_map/ppermute | solution.py:288
  35.5 0.8 %add_multiply_fusion = f32[128,512]{1,0:T(8,128)} fusion(bf16[128,512]{1,0:T(8,128)(2,1)S(1)} %collective-permute-done.7, f32[128,512]{1,0:T(8,128)S(1)} %get-tuple-element.64, bf16[128,512]{1,0:T(8,128)(2,1)S(1)} %collective-permute-done.12), kind=kLoop, calls=%fused_computation | loop fusion | flops 327680 | bytes 786432 | tf_op jit(solution)/shard_map/mul | solution.py:338
  (15 shorter events, 0.1 us)
Async XLA Ops:
  0.6 14.6 %copy-start.1 = (bf16[128,512]{1,0:T(8,128)(2,1)S(1)}, bf16[128,512]{1,0:T(8,128)(2,1)}, u32[]{:S(2)}) copy-start(bf16[128,512]{1,0:T(8,128)(2,1)} %refs_4_.5) | copy-start | bytes 393220
  0.6 13.1 %copy-start.4 = (s32[1,64]{1,0:T(1,128)S(1)}, s32[1,64]{1,0:T(1,128)}, u32[]{:S(2)}) copy-start(s32[1,64]{1,0:T(1,128)} %ts_ref.1) | copy-start | bytes 772
  0.7 13.1 %copy-start.3 = (s32[1,64]{1,0:T(1,128)S(1)}, s32[1,64]{1,0:T(1,128)}, u32[]{:S(2)}) copy-start(s32[1,64]{1,0:T(1,128)} %tf_ref.1) | copy-start | bytes 772
  0.7 14.6 %copy-start.2 = (s32[1024]{0:T(1024)S(1)}, s32[1024]{0:T(1024)}, u32[]{:S(2)}) copy-start(s32[1024]{0:T(1024)} %param.10) | copy-start | bytes 12292
  0.7 10.7 %collective-permute-start.1 = (bf16[128,512]{1,0:T(8,128)(2,1)}, bf16[128,512]{1,0:T(8,128)(2,1)S(1)}, u32[]{:S(2)}, u32[]{:S(2)}) collective-permute-start(bf16[128,512]{1,0:T(8,128)(2,1)} %refs_4_.5), channel_id=1, source_target_pairs={{0,4},{1,5},{2,6},{3,7},{4,0},{5,1},{6,2},{7,3},{8,12},{9,13},{10,... | collective-permute-start | bytes 393224 | tf_op jit(solution)/shard_map/ppermute | solution.py:288
  4.8 6.8 %collective-permute-start = (bf16[128,512]{1,0:T(8,128)(2,1)}, bf16[128,512]{1,0:T(8,128)(2,1)S(1)}, u32[]{:S(2)}, u32[]{:S(2)}) collective-permute-start(bf16[128,512]{1,0:T(8,128)(2,1)} %refs_4_.5), channel_id=1, source_target_pairs={{0,2},{1,3},{2,0},{3,1},{4,6},{5,7},{6,4},{7,5},{8,10},{9,11},{10,... | collective-permute-start | bytes 393224 | tf_op jit(solution)/shard_map/ppermute | solution.py:288
  11.6 3.6 %collective-permute-start.2 = (bf16[1024,512]{1,0:T(8,128)(2,1)S(1)}, bf16[1024,512]{1,0:T(8,128)(2,1)S(1)}, u32[]{:S(2)}, u32[]{:S(2)}) collective-permute-start(bf16[1024,512]{1,0:T(8,128)(2,1)S(1)} %embed.1.refs_0_.refs_2_), channel_id=1, source_target_pairs={{0,1},{1,0},{2,3},{3,2},{4,5},{5,4},{6,7},{7,6},{8,9},{9,8},{10,11... | collective-permute-start | bytes 3145736 | tf_op jit(solution)/shard_map/ppermute | solution.py:288
  11.6 5.9 %collective-permute-start.4 = (bf16[128,512]{1,0:T(8,128)(2,1)S(1)}, bf16[128,512]{1,0:T(8,128)(2,1)S(1)}, u32[]{:S(2)}, u32[]{:S(2)}) collective-permute-start(bf16[128,512]{1,0:T(8,128)(2,1)S(1)} %collective-permute-done.1.refs_5_), channel_id=1, source_target_pairs={{0,2},{1,3},{2,0},{3,1},{4,6},{5,7},{6,4},{7,5},{8,10},{9,11},{10,... | collective-permute-start | bytes 393224 | tf_op jit(solution)/shard_map/ppermute | solution.py:288
  14.0 1.2 %collective-permute-start.3 = (f32[4,1024]{1,0:T(4,128)S(1)}, f32[4,1024]{1,0:T(4,128)S(1)}, u32[]{:S(2)}, u32[]{:S(2)}) collective-permute-start(f32[4,1024]{1,0:T(4,128)S(1)} %get-tuple-element.37), channel_id=1, source_target_pairs={{0,1},{1,0},{2,3},{3,2},{4,5},{5,4},{6,7},{7,6},{8,9},{9,8},{10,11... | collective-permute-start | bytes 49160 | tf_op jit(solution)/shard_map/ppermute | solution.py:288
  18.4 1.2 %collective-permute-start.5 = (f32[2,2048]{1,0:T(2,128)S(1)}, f32[2,2048]{1,0:T(2,128)S(1)}, u32[]{:S(2)}, u32[]{:S(2)}) collective-permute-start(f32[2,2048]{1,0:T(2,128)S(1)} %get-tuple-element.42.refs_0_), channel_id=1, source_target_pairs={{0,1},{1,0},{2,3},{3,2},{4,5},{5,4},{6,7},{7,6},{8,9},{9,8},{10,11... | collective-permute-start | bytes 49160 | tf_op jit(solution)/shard_map/ppermute | solution.py:288
  20.1 5.6 %collective-permute-start.6 = (bf16[128,512]{1,0:T(8,128)(2,1)S(1)}, bf16[128,512]{1,0:T(8,128)(2,1)S(1)}, u32[]{:S(2)}, u32[]{:S(2)}) collective-permute-start(bf16[128,512]{1,0:T(8,128)(2,1)S(1)} %get-tuple-element.54), channel_id=1, source_target_pairs={{0,2},{1,3},{2,0},{3,1},{4,6},{5,7},{6,4},{7,5},{8,10},{9,11},{10,... | collective-permute-start | bytes 393224 | tf_op jit(solution)/shard_map/ppermute | solution.py:288
  23.8 2.0 %collective-permute-start.8 = (bf16[256,512]{1,0:T(8,128)(2,1)S(1)}, bf16[256,512]{1,0:T(8,128)(2,1)S(1)}, u32[]{:S(2)}, u32[]{:S(2)}) collective-permute-start(bf16[256,512]{1,0:T(8,128)(2,1)S(1)} %get-tuple-element.59), channel_id=1, source_target_pairs={{0,1},{1,0},{2,3},{3,2},{4,5},{5,4},{6,7},{7,6},{8,9},{9,8},{10,11... | collective-permute-start | bytes 786440 | tf_op jit(solution)/shard_map/ppermute | solution.py:288
  23.9 11.6 %collective-permute-start.12 = (bf16[128,512]{1,0:T(8,128)(2,1)S(1)}, bf16[128,512]{1,0:T(8,128)(2,1)S(1)}, u32[]{:S(2)}, u32[]{:S(2)}) collective-permute-start(bf16[128,512]{1,0:T(8,128)(2,1)S(1)} %get-tuple-element.65), channel_id=1, source_target_pairs={{0,2},{1,3},{2,0},{3,1},{4,6},{5,7},{6,4},{7,5},{8,10},{9,11},{10,... | collective-permute-start | bytes 393224 | tf_op jit(solution)/shard_map/ppermute | solution.py:288
  24.5 4.1 %collective-permute-start.9 = (bf16[256,512]{1,0:T(8,128)(2,1)S(1)}, bf16[256,512]{1,0:T(8,128)(2,1)S(1)}, u32[]{:S(2)}, u32[]{:S(2)}) collective-permute-start(bf16[256,512]{1,0:T(8,128)(2,1)S(1)} %get-tuple-element.60), channel_id=1, source_target_pairs={{0,1},{1,0},{2,3},{3,2},{4,5},{5,4},{6,7},{7,6},{8,9},{9,8},{10,11... | collective-permute-start | bytes 786440 | tf_op jit(solution)/shard_map/ppermute | solution.py:288
  24.7 4.0 %collective-permute-start.10 = (bf16[256,512]{1,0:T(8,128)(2,1)S(1)}, bf16[256,512]{1,0:T(8,128)(2,1)S(1)}, u32[]{:S(2)}, u32[]{:S(2)}) collective-permute-start(bf16[256,512]{1,0:T(8,128)(2,1)S(1)} %get-tuple-element.61), channel_id=1, source_target_pairs={{0,1},{1,0},{2,3},{3,2},{4,5},{5,4},{6,7},{7,6},{8,9},{9,8},{10,11... | collective-permute-start | bytes 786440 | tf_op jit(solution)/shard_map/ppermute | solution.py:288
  25.7 3.0 %collective-permute-start.11 = (bf16[256,512]{1,0:T(8,128)(2,1)S(1)}, bf16[256,512]{1,0:T(8,128)(2,1)S(1)}, u32[]{:S(2)}, u32[]{:S(2)}) collective-permute-start(bf16[256,512]{1,0:T(8,128)(2,1)S(1)} %get-tuple-element.62), channel_id=1, source_target_pairs={{0,1},{1,0},{2,3},{3,2},{4,5},{5,4},{6,7},{7,6},{8,9},{9,8},{10,11... | collective-permute-start | bytes 786440 | tf_op jit(solution)/shard_map/ppermute | solution.py:288
  25.8 2.9 %copy-start = (bf16[1024,512]{1,0:T(8,128)(2,1)S(1)}, bf16[1024,512]{1,0:T(8,128)(2,1)}, u32[]{:S(2)}) copy-start(bf16[1024,512]{1,0:T(8,128)(2,1)} %refs_1_.1) | copy-start | bytes 3145732
  25.8 9.7 %collective-permute-start.7 = (bf16[128,512]{1,0:T(8,128)(2,1)S(1)}, bf16[128,512]{1,0:T(8,128)(2,1)S(1)}, u32[]{:S(2)}, u32[]{:S(2)}) collective-permute-start(bf16[128,512]{1,0:T(8,128)(2,1)S(1)} %add_convert_fusion), channel_id=1, source_target_pairs={{0,4},{1,5},{2,6},{3,7},{4,0},{5,1},{6,2},{7,3},{8,12},{9,13},{10,... | collective-permute-start | bytes 393224 | tf_op jit(solution)/shard_map/ppermute | solution.py:288
where the time goes:
time: 36.4 us; the launch traced here: 36.2 us
  starting transfers between devices  12.3 us (34%)
  Pallas kernels  11.2 us (31%)
  waiting for transfers between devices  10.4 us (29%)
  between operations  1.46 us (4%)
  other arithmetic  0.79 us (2%)
    ppermute x13, starting transfers between devices, trade(): return lax.ppermute(x, 'vid', [(i, i ^ k) for i in range(videos)])  12.3 us
    ppermute x13, waiting for transfers between devices, trade(): return lax.ppermute(x, 'vid', [(i, i ^ k) for i in range(videos)])  10.4 us
    pallas_call x1, Pallas kernels, embed(): pl.pallas_call(embed_kernel, in_specs=[ANYWHERE, ANYWHERE], out_specs=VME...  3.18 us
    pallas_call x2, Pallas kernels, score(): pl.pallas_call(lambda *refs: score_kernel(ks, temper, *refs), in_specs=[V...  2.26 us
    pallas_call x1, Pallas kernels, back(): pl.pallas_call(lambda *refs: back_kernel(temper, *refs), in_specs=[VMEM]...  2.13 us
    pallas_call x2, Pallas kernels, share(): pl.pallas_call(lambda *refs: share_kernel(ks, *refs), in_specs=[VMEM] * (...  1.9 us
    pallas_call x2, Pallas kernels, rows_of(): pl.pallas_call(lambda *refs: rows_kernel(n, rows if theirs else 0, *refs)...  1.48 us
    mul x1, other arithmetic, shards(): return (loss[0].reshape(-1), frame_grad, sums[0] * temper)  0.76 us
  transfers between devices with their start and end apart: 13, of which 7 were waited for; matrix products, arithmetic and copies ran while one was open for 0% of the time, Pallas kernels for 27%

commit v1 on v0

--- a/solution.py
+++ b/solution.py
@@ -276,6 +276,35 @@
     )(mine, w, *gots)
 
 
+def finish_kernel(temper, *refs):
+    own_ref, *come_refs, out_hbm, out_ref, sem = refs
+    tile = out_ref.shape[0] // TILES
+    writes = []
+    for n in range(TILES):
+        at = slice(n * tile, (n + 1) * tile)
+        total = own_ref[at, :]
+        for come_ref in come_refs:
+            total = total + come_ref[at, :].astype(F32)
+        out_ref[at, :] = total * temper
+        cut = pl.ds(n * tile, tile)
+        writes.append(pltpu.make_async_copy(out_ref.at[cut], out_hbm.at[cut], sem.at[n]))
+        writes[n].start()
+    for write in writes:
+        write.wait()
+
+
+def finish(own, come, temper):
+    return pl.pallas_call(
+        lambda *refs: finish_kernel(temper, *refs),
+        in_specs=[VMEM] * (1 + len(come)),
+        out_specs=ANYWHERE,
+        out_shape=jax.ShapeDtypeStruct(own.shape, F32),
+        scratch_shapes=[pltpu.VMEM(own.shape, F32), pltpu.SemaphoreType.DMA((TILES,))],
+        compiler_params=params(24),
+        name="finish",
+    )(own, *come)
+
+
 def shards(frames, w_frame, step_emb, targets, tile_frame, tile_step, tile_count):
     videos = lax.axis_size("vid")
     chips = videos // 2
@@ -327,15 +356,18 @@
     lent = [trade(piece, 1) for piece in rows_of(*parts, True)]
     (own_rows,) = rows_of(*parts, False)
     frame_grad = back(own_rows, lent, w_frame, temper)
-    bit = 1
+    bit, ends = 1, []
     while bit < chips:
         for k in range(chips - bit, 0, -2 * bit):
             come = trade(sums[k].astype(BF16), 2 * bit)
-            if 2 * bit == chips:
-                come, frame_grad = lax.optimization_barrier((come, frame_grad))
-            sums[k - bit] = sums[k - bit].astype(F32) + come.astype(F32)
+            if k == bit:
+                ends.append(come)
+            else:
+                sums[k - bit] = sums[k - bit].astype(F32) + come.astype(F32)
         bit *= 2
-    return (loss[0].reshape(-1), frame_grad, sums[0] * temper)
+    *ends, frame_grad = lax.optimization_barrier((*ends, frame_grad))
+    step_grad = finish(sums[0], ends, temper)
+    return (loss[0].reshape(-1), frame_grad, step_grad)
 
 
 def solution(mesh):

time: 36.4 us -> 36.4 us (level)
  Pallas kernels: 11.2 us -> 12 us
  other arithmetic: 0.79 us -> 0.03 us
    mul x1 -> x0, other arithmetic: 0.76 us -> none  [shards(): return (loss[0].reshape(-1), frame_grad, sums[0] * temper)]
    pallas_call x0 -> x1, Pallas kernels: none -> 0.74 us  [finish(): pl.pallas_call(lambda *refs: finish_kernel(temper, *refs), in_specs=[VMEM...]
where the time goes in v1:
time: 36.4 us; the launch traced here: 36.2 us
  starting transfers between devices  12.3 us (34%)
  Pallas kernels  12 us (33%)
  waiting for transfers between devices  10.4 us (29%)
  between operations  1.46 us (4%)
    ppermute x13, starting transfers between devices, trade(): return lax.ppermute(x, 'vid', [(i, i ^ k) for i in range(videos)])  12.3 us
    ppermute x13, waiting for transfers between devices, trade(): return lax.ppermute(x, 'vid', [(i, i ^ k) for i in range(videos)])  10.4 us
    pallas_call x1, Pallas kernels, embed(): pl.pallas_call(embed_kernel, in_specs=[ANYWHERE, ANYWHERE], out_specs=VME...  3.18 us
    pallas_call x2, Pallas kernels, score(): pl.pallas_call(lambda *refs: score_kernel(ks, temper, *refs), in_specs=[V...  2.26 us
    pallas_call x1, Pallas kernels, back(): pl.pallas_call(lambda *refs: back_kernel(temper, *refs), in_specs=[VMEM]...  2.13 us
    pallas_call x2, Pallas kernels, share(): pl.pallas_call(lambda *refs: share_kernel(ks, *refs), in_specs=[VMEM] * (...  1.9 us
    pallas_call x2, Pallas kernels, rows_of(): pl.pallas_call(lambda *refs: rows_kernel(n, rows if theirs else 0, *refs)...  1.48 us
    pallas_call x1, Pallas kernels, finish(): pl.pallas_call(lambda *refs: finish_kernel(temper, *refs), in_specs=[VMEM...  0.74 us
  transfers between devices with their start and end apart: 13, of which 7 were waited for; matrix products, arithmetic and copies ran while one was open for 0% of the time, Pallas kernels for 27%

profile of v1, /device:TPU:0, one launch (start us, length us, event | category | flops | bytes accessed | tf_op | source)
XLA Modules:
  0.0 36.2 jit_solution(12842752795409444390)
XLA Ops:
  0.7 4.1 %collective-permute-start.1 = (bf16[128,512]{1,0:T(8,128)(2,1)}, bf16[128,512]{1,0:T(8,128)(2,1)S(1)}, u32[]{:S(2)}, u32[]{:S(2)}) collective-permute-start(bf16[128,512]{1,0:T(8,128)(2,1)} %refs_4_.5), channel_id=1, source_target_pairs={{0,4},{1,5},{2,6},{3,7},{4,0},{5,1},{6,2},{7,3},{8,12},{9,13},{10,... | collective-permute-start | bytes 393224 | tf_op jit(solution)/shard_map/ppermute | solution.py:317
  4.8 1.6 %collective-permute-start = (bf16[128,512]{1,0:T(8,128)(2,1)}, bf16[128,512]{1,0:T(8,128)(2,1)S(1)}, u32[]{:S(2)}, u32[]{:S(2)}) collective-permute-start(bf16[128,512]{1,0:T(8,128)(2,1)} %refs_4_.5), channel_id=1, source_target_pairs={{0,2},{1,3},{2,0},{3,1},{4,6},{5,7},{6,4},{7,5},{8,10},{9,11},{10,... | collective-permute-start | bytes 393224 | tf_op jit(solution)/shard_map/ppermute | solution.py:317
  6.3 3.2 %embed.1.refs_0_.refs_2_ = bf16[1024,512]{1,0:T(8,128)(2,1)S(1)} custom-call(bf16[1024,1024]{1,0:T(8,128)(2,1)} %x_hbm.1, bf16[1024,512]{1,0:T(8,128)(2,1)} %refs_1_.1), custom_call_target="tpu_custom_call" | custom-call | flops 1073741824 | bytes 4194304 | tf_op jit(solution)/shard_map/embed/pallas_call | solution.py:55
  9.5 1.9 %collective-permute-done.1.refs_5_ = bf16[128,512]{1,0:T(8,128)(2,1)S(1)} collective-permute-done((bf16[128,512]{1,0:T(8,128)(2,1)}, bf16[128,512]{1,0:T(8,128)(2,1)S(1)}, u32[]{:S(2)}, u32[]{:S(2)}) %collective-permute-start.1) | collective-permute-done | bytes 131104 | tf_op jit(solution)/shard_map/ppermute | solution.py:317
  11.4 0.2 collective-permute-done.refs_6_
  11.6 0.0 collective-permute-start.2
  11.6 1.4 %collective-permute-start.4 = (bf16[128,512]{1,0:T(8,128)(2,1)S(1)}, bf16[128,512]{1,0:T(8,128)(2,1)S(1)}, u32[]{:S(2)}, u32[]{:S(2)}) collective-permute-start(bf16[128,512]{1,0:T(8,128)(2,1)S(1)} %collective-permute-done.1.refs_5_), channel_id=1, source_target_pairs={{0,2},{1,3},{2,0},{3,1},{4,6},{5,7},{6,4},{7,5},{8,10},{9,11},{10,... | collective-permute-start | bytes 393224 | tf_op jit(solution)/shard_map/ppermute | solution.py:317
  13.7 0.3 sight.1
  14.0 0.3 collective-permute-start.3
  14.3 1.0 %collective-permute-done.3.refs_3_ = f32[4,1024]{1,0:T(4,128)S(1)} collective-permute-done((f32[4,1024]{1,0:T(4,128)S(1)}, f32[4,1024]{1,0:T(4,128)S(1)}, u32[]{:S(2)}, u32[]{:S(2)}) %collective-permute-start.3) | collective-permute-done | bytes 16416 | tf_op jit(solution)/shard_map/ppermute | solution.py:317
  15.2 1.4 %score_1.1 = (f32[128,2048]{1,0:T(8,128)S(1)}, f32[128,2048]{1,0:T(8,128)S(1)}, f32[128,2048]{1,0:T(8,128)S(1)}, f32[1,2048]{1,0:T(1,128)S(1)}, f32[2,2048]{1,0:T(2,128)S(1)}, /*index=5*/f32[1,1024]{1,0:T(1,128)S(1)}) custom-call(bf16[1024,512]{1,0:T(8,128)(2,1)S(1)} %embed.1.refs_0_.refs_2_, bf16[1024,512]{1,0:T(8,128)(2,1)S(1)} %collective-permute-done.2.refs_1_.refs_3_, ...), custom_call_target="tpu_custom_call" | custom-call | flops 805306368 | bytes 5242880 | tf_op jit(solution)/shard_map/score_1/pallas_call | solution.py:144
  16.6 0.9 %collective-permute-done.4.refs_4_.refs_7_ = bf16[128,512]{1,0:T(8,128)(2,1)S(1)} collective-permute-done((bf16[128,512]{1,0:T(8,128)(2,1)S(1)}, bf16[128,512]{1,0:T(8,128)(2,1)S(1)}, u32[]{:S(2)}, u32[]{:S(2)}) %collective-permute-start.4) | collective-permute-done | bytes 131104 | tf_op jit(solution)/shard_map/ppermute | solution.py:317
  17.5 0.9 %score_3.1 = (f32[128,2048]{1,0:T(8,128)S(1)}, f32[1,2048]{1,0:T(1,128)S(1)}, f32[2,2048]{1,0:T(2,128)S(1)}) custom-call(bf16[1024,512]{1,0:T(8,128)(2,1)S(1)} %embed.1.refs_0_.refs_2_, bf16[1024,512]{1,0:T(8,128)(2,1)S(1)} %collective-permute-done.2.refs_1_.refs_3_, f32[4,1024]{1,0:T(4,128)S(1)} %get-tuple-element.37.refs_2_, ...), custom_call_target="tpu_custom_call" | custom-call | flops 268435456 | bytes 3145728 | tf_op jit(solution)/shard_map/score_3/pallas_call | solution.py:144
  18.4 0.1 collective-permute-start.5
  18.5 1.2 %collective-permute-done.5.refs_1_ = f32[2,2048]{1,0:T(2,128)S(1)} collective-permute-done((f32[2,2048]{1,0:T(2,128)S(1)}, f32[2,2048]{1,0:T(2,128)S(1)}, u32[]{:S(2)}, u32[]{:S(2)}) %collective-permute-start.5) | collective-permute-done | bytes 16416 | tf_op jit(solution)/shard_map/ppermute | solution.py:317
  19.6 0.4 %share_3.1 = (bf16[128,2048]{1,0:T(8,128)(2,1)S(1)}, bf16[128,512]{1,0:T(8,128)(2,1)S(1)}) custom-call(f32[2,2048]{1,0:T(2,128)S(1)} %get-tuple-element.43.refs_0_, f32[2,2048]{1,0:T(2,128)S(1)} %collective-permute-done.5.refs_1_, bf16[1024,512]{1,0:T(8,128)(2,1)S(1)} %embed.1.refs_0_.refs_2_, bf16[1024,512]{1,0:T(8,128)(2,1)S(1)} %collective-permute-done.2.refs_1_.refs_3_, ...), custom_call_target="tpu_custom_call" | custom-call | flops 268435456 | bytes 3670016 | tf_op jit(solution)/shard_map/share_3/pallas_call | solution.py:200
  20.1 1.5 %collective-permute-start.7 = (bf16[128,512]{1,0:T(8,128)(2,1)S(1)}, bf16[128,512]{1,0:T(8,128)(2,1)S(1)}, u32[]{:S(2)}, u32[]{:S(2)}) collective-permute-start(bf16[128,512]{1,0:T(8,128)(2,1)S(1)} %get-tuple-element.56), channel_id=1, source_target_pairs={{0,2},{1,3},{2,0},{3,1},{4,6},{5,7},{6,4},{7,5},{8,10},{9,11},{10,... | collective-permute-start | bytes 393224 | tf_op jit(solution)/shard_map/ppermute | solution.py:317
  21.6 1.5 %share_2.1 = (bf16[128,2048]{1,0:T(8,128)(2,1)S(1)}, bf16[128,2048]{1,0:T(8,128)(2,1)S(1)}, bf16[128,2048]{1,0:T(8,128)(2,1)S(1)}, f32[128,512]{1,0:T(8,128)S(1)...) custom-call(f32[2,2048]{1,0:T(2,128)S(1)} %get-tuple-element.43.refs_0_, ...), custom_call_target="tpu_custom_call" | custom-call | flops 805306368 | bytes 6815744 | tf_op jit(solution)/shard_map/share_2/pallas_call | solution.py:200
  23.1 0.7 %rows_theirs.1 = (bf16[256,512]{1,0:T(8,128)(2,1)S(1)}, bf16[256,512]{1,0:T(8,128)(2,1)S(1)}, bf16[256,512]{1,0:T(8,128)(2,1)S(1)}, bf16[256,512]{1,0:T(8,128)(2,1)S(1)}) custom-call(bf16[128,2048]{1,0:T(8,128)(2,1)S(1)} %get-tuple-element.57.refs_0_, bf16[128,2048]{1,0:T(8,128)(2,1)S(1)} %get-tuple-element.58.refs_1_, ...), custom_call_target="tpu_custom_call" | custom-call | flops 536870912 | bytes 2621440 | tf_op jit(solution)/shard_map/rows_theirs/pallas_call | solution.py:232
  23.8 0.1 collective-permute-start.9
  23.9 0.6 %collective-permute-start.6 = (bf16[128,512]{1,0:T(8,128)(2,1)S(1)}, bf16[128,512]{1,0:T(8,128)(2,1)S(1)}, u32[]{:S(2)}, u32[]{:S(2)}) collective-permute-start(bf16[128,512]{1,0:T(8,128)(2,1)S(1)} %get-tuple-element.54), channel_id=1, source_target_pairs={{0,2},{1,3},{2,0},{3,1},{4,6},{5,7},{6,4},{7,5},{8,10},{9,11},{10,... | collective-permute-start | bytes 393224 | tf_op jit(solution)/shard_map/ppermute | solution.py:317
  24.5 0.2 collective-permute-start.10
  24.7 0.3 collective-permute-start.11
  25.1 0.7 %collective-permute-done.7 = bf16[128,512]{1,0:T(8,128)(2,1)S(1)} collective-permute-done((bf16[128,512]{1,0:T(8,128)(2,1)S(1)}, bf16[128,512]{1,0:T(8,128)(2,1)S(1)}, u32[]{:S(2)}, u32[]{:S(2)}) %collective-permute-start.7) | collective-permute-done | bytes 131104 | tf_op jit(solution)/shard_map/ppermute | solution.py:317
  25.7 0.0 collective-permute-start.12
  25.8 0.0 copy-start
  25.8 0.0 collective-permute-done.9.refs_2_
  25.8 2.1 %collective-permute-start.8 = (bf16[128,512]{1,0:T(8,128)(2,1)S(1)}, bf16[128,512]{1,0:T(8,128)(2,1)S(1)}, u32[]{:S(2)}, u32[]{:S(2)}) collective-permute-start(bf16[128,512]{1,0:T(8,128)(2,1)S(1)} %add_convert_fusion), channel_id=1, source_target_pairs={{0,4},{1,5},{2,6},{3,7},{4,0},{5,1},{6,2},{7,3},{8,12},{9,13},{10,... | collective-permute-start | bytes 393224 | tf_op jit(solution)/shard_map/ppermute | solution.py:317
  27.9 0.7 %rows_mine.1.refs_0_ = f32[1024,512]{1,0:T(8,128)S(1)} custom-call(bf16[128,2048]{1,0:T(8,128)(2,1)S(1)} %get-tuple-element.57.refs_0_, bf16[128,2048]{1,0:T(8,128)(2,1)S(1)} %get-tuple-element.58.refs_1_, bf16[128,2048]{1,0:T(8,128)(2,1)S(1)} %get-tuple-element.59.refs_2_, bf16[128,2048]{1,0:T(8,128)(2,1)S(1)} %get-tuple-element.60.refs_3_, ...), custom_call_target="tpu_custom_call" | custom-call | flops 536870912 | bytes 2621440 | tf_op jit(solution)/shard_map/rows_mine/pallas_call | solution.py:232
  28.7 2.1 %back.1 = bf16[1024,1024]{1,0:T(8,128)(2,1)} custom-call(f32[1024,512]{1,0:T(8,128)S(1)} %rows_mine.1.refs_0_, bf16[1024,512]{1,0:T(8,128)(2,1)S(1)} %copy-done, bf16[256,512]{1,0:T(8,128)(2,1)S(1)} %collective-permute-done.9.refs_2_, bf16[256,512]{1,0:T(8,128)(2,1)S(1)} %collective-permute-done.10.refs_3_, ...), custom_call_target="tpu_custom_call" | custom-call | flops 1073741824 | bytes 3145728 | tf_op jit(solution)/shard_map/back/pallas_call | solution.py:264
  30.9 4.6 %collective-permute-done.8.refs_2_ = bf16[128,512]{1,0:T(8,128)(2,1)S(1)} collective-permute-done((bf16[128,512]{1,0:T(8,128)(2,1)S(1)}, bf16[128,512]{1,0:T(8,128)(2,1)S(1)}, u32[]{:S(2)}, u32[]{:S(2)}) %collective-permute-start.8) | collective-permute-done | bytes 131104 | tf_op jit(solution)/shard_map/ppermute | solution.py:317
  35.5 0.7 %finish.1 = f32[128,512]{1,0:T(8,128)} custom-call(f32[128,512]{1,0:T(8,128)S(1)} %get-tuple-element.66.refs_0_, bf16[128,512]{1,0:T(8,128)(2,1)S(1)} %collective-permute-done.6.refs_1_, bf16[128,512]{1,0:T(8,128)(2,1)S(1)} %collective-permute-done.8.refs_2_), custom_call_target="tpu_custom_call" | custom-call | tf_op jit(solution)/shard_map/finish/pallas_call | solution.py:297
  (15 shorter events, 0.1 us)
Async XLA Ops:
  0.6 14.6 %copy-start.1 = (bf16[128,512]{1,0:T(8,128)(2,1)S(1)}, bf16[128,512]{1,0:T(8,128)(2,1)}, u32[]{:S(2)}) copy-start(bf16[128,512]{1,0:T(8,128)(2,1)} %refs_4_.5) | copy-start | bytes 393220
  0.6 13.1 %copy-start.4 = (s32[1,64]{1,0:T(1,128)S(1)}, s32[1,64]{1,0:T(1,128)}, u32[]{:S(2)}) copy-start(s32[1,64]{1,0:T(1,128)} %ts_ref.1) | copy-start | bytes 772
  0.7 13.1 %copy-start.3 = (s32[1,64]{1,0:T(1,128)S(1)}, s32[1,64]{1,0:T(1,128)}, u32[]{:S(2)}) copy-start(s32[1,64]{1,0:T(1,128)} %tf_ref.1) | copy-start | bytes 772
  0.7 14.6 %copy-start.2 = (s32[1024]{0:T(1024)S(1)}, s32[1024]{0:T(1024)}, u32[]{:S(2)}) copy-start(s32[1024]{0:T(1024)} %param.10) | copy-start | bytes 12292
  0.7 10.7 %collective-permute-start.1 = (bf16[128,512]{1,0:T(8,128)(2,1)}, bf16[128,512]{1,0:T(8,128)(2,1)S(1)}, u32[]{:S(2)}, u32[]{:S(2)}) collective-permute-start(bf16[128,512]{1,0:T(8,128)(2,1)} %refs_4_.5), channel_id=1, source_target_pairs={{0,4},{1,5},{2,6},{3,7},{4,0},{5,1},{6,2},{7,3},{8,12},{9,13},{10,... | collective-permute-start | bytes 393224 | tf_op jit(solution)/shard_map/ppermute | solution.py:317
  4.8 6.8 %collective-permute-start = (bf16[128,512]{1,0:T(8,128)(2,1)}, bf16[128,512]{1,0:T(8,128)(2,1)S(1)}, u32[]{:S(2)}, u32[]{:S(2)}) collective-permute-start(bf16[128,512]{1,0:T(8,128)(2,1)} %refs_4_.5), channel_id=1, source_target_pairs={{0,2},{1,3},{2,0},{3,1},{4,6},{5,7},{6,4},{7,5},{8,10},{9,11},{10,... | collective-permute-start | bytes 393224 | tf_op jit(solution)/shard_map/ppermute | solution.py:317
  11.6 3.6 %collective-permute-start.2 = (bf16[1024,512]{1,0:T(8,128)(2,1)S(1)}, bf16[1024,512]{1,0:T(8,128)(2,1)S(1)}, u32[]{:S(2)}, u32[]{:S(2)}) collective-permute-start(bf16[1024,512]{1,0:T(8,128)(2,1)S(1)} %embed.1.refs_0_.refs_2_), channel_id=1, source_target_pairs={{0,1},{1,0},{2,3},{3,2},{4,5},{5,4},{6,7},{7,6},{8,9},{9,8},{10,11... | collective-permute-start | bytes 3145736 | tf_op jit(solution)/shard_map/ppermute | solution.py:317
  11.6 5.9 %collective-permute-start.4 = (bf16[128,512]{1,0:T(8,128)(2,1)S(1)}, bf16[128,512]{1,0:T(8,128)(2,1)S(1)}, u32[]{:S(2)}, u32[]{:S(2)}) collective-permute-start(bf16[128,512]{1,0:T(8,128)(2,1)S(1)} %collective-permute-done.1.refs_5_), channel_id=1, source_target_pairs={{0,2},{1,3},{2,0},{3,1},{4,6},{5,7},{6,4},{7,5},{8,10},{9,11},{10,... | collective-permute-start | bytes 393224 | tf_op jit(solution)/shard_map/ppermute | solution.py:317
  14.0 1.2 %collective-permute-start.3 = (f32[4,1024]{1,0:T(4,128)S(1)}, f32[4,1024]{1,0:T(4,128)S(1)}, u32[]{:S(2)}, u32[]{:S(2)}) collective-permute-start(f32[4,1024]{1,0:T(4,128)S(1)} %get-tuple-element.38), channel_id=1, source_target_pairs={{0,1},{1,0},{2,3},{3,2},{4,5},{5,4},{6,7},{7,6},{8,9},{9,8},{10,11... | collective-permute-start | bytes 49160 | tf_op jit(solution)/shard_map/ppermute | solution.py:317
  18.4 1.2 %collective-permute-start.5 = (f32[2,2048]{1,0:T(2,128)S(1)}, f32[2,2048]{1,0:T(2,128)S(1)}, u32[]{:S(2)}, u32[]{:S(2)}) collective-permute-start(f32[2,2048]{1,0:T(2,128)S(1)} %get-tuple-element.43.refs_0_), channel_id=1, source_target_pairs={{0,1},{1,0},{2,3},{3,2},{4,5},{5,4},{6,7},{7,6},{8,9},{9,8},{10,11... | collective-permute-start | bytes 49160 | tf_op jit(solution)/shard_map/ppermute | solution.py:317
  20.1 5.6 %collective-permute-start.7 = (bf16[128,512]{1,0:T(8,128)(2,1)S(1)}, bf16[128,512]{1,0:T(8,128)(2,1)S(1)}, u32[]{:S(2)}, u32[]{:S(2)}) collective-permute-start(bf16[128,512]{1,0:T(8,128)(2,1)S(1)} %get-tuple-element.56), channel_id=1, source_target_pairs={{0,2},{1,3},{2,0},{3,1},{4,6},{5,7},{6,4},{7,5},{8,10},{9,11},{10,... | collective-permute-start | bytes 393224 | tf_op jit(solution)/shard_map/ppermute | solution.py:317
  23.8 2.0 %collective-permute-start.9 = (bf16[256,512]{1,0:T(8,128)(2,1)S(1)}, bf16[256,512]{1,0:T(8,128)(2,1)S(1)}, u32[]{:S(2)}, u32[]{:S(2)}) collective-permute-start(bf16[256,512]{1,0:T(8,128)(2,1)S(1)} %get-tuple-element.61), channel_id=1, source_target_pairs={{0,1},{1,0},{2,3},{3,2},{4,5},{5,4},{6,7},{7,6},{8,9},{9,8},{10,11... | collective-permute-start | bytes 786440 | tf_op jit(solution)/shard_map/ppermute | solution.py:317
  23.9 7.0 %collective-permute-start.6 = (bf16[128,512]{1,0:T(8,128)(2,1)S(1)}, bf16[128,512]{1,0:T(8,128)(2,1)S(1)}, u32[]{:S(2)}, u32[]{:S(2)}) collective-permute-start(bf16[128,512]{1,0:T(8,128)(2,1)S(1)} %get-tuple-element.54), channel_id=1, source_target_pairs={{0,2},{1,3},{2,0},{3,1},{4,6},{5,7},{6,4},{7,5},{8,10},{9,11},{10,... | collective-permute-start | bytes 393224 | tf_op jit(solution)/shard_map/ppermute | solution.py:317
  24.5 4.1 %collective-permute-start.10 = (bf16[256,512]{1,0:T(8,128)(2,1)S(1)}, bf16[256,512]{1,0:T(8,128)(2,1)S(1)}, u32[]{:S(2)}, u32[]{:S(2)}) collective-permute-start(bf16[256,512]{1,0:T(8,128)(2,1)S(1)} %get-tuple-element.62), channel_id=1, source_target_pairs={{0,1},{1,0},{2,3},{3,2},{4,5},{5,4},{6,7},{7,6},{8,9},{9,8},{10,11... | collective-permute-start | bytes 786440 | tf_op jit(solution)/shard_map/ppermute | solution.py:317
  24.7 4.0 %collective-permute-start.11 = (bf16[256,512]{1,0:T(8,128)(2,1)S(1)}, bf16[256,512]{1,0:T(8,128)(2,1)S(1)}, u32[]{:S(2)}, u32[]{:S(2)}) collective-permute-start(bf16[256,512]{1,0:T(8,128)(2,1)S(1)} %get-tuple-element.63), channel_id=1, source_target_pairs={{0,1},{1,0},{2,3},{3,2},{4,5},{5,4},{6,7},{7,6},{8,9},{9,8},{10,11... | collective-permute-start | bytes 786440 | tf_op jit(solution)/shard_map/ppermute | solution.py:317
  25.7 3.0 %collective-permute-start.12 = (bf16[256,512]{1,0:T(8,128)(2,1)S(1)}, bf16[256,512]{1,0:T(8,128)(2,1)S(1)}, u32[]{:S(2)}, u32[]{:S(2)}) collective-permute-start(bf16[256,512]{1,0:T(8,128)(2,1)S(1)} %get-tuple-element.64), channel_id=1, source_target_pairs={{0,1},{1,0},{2,3},{3,2},{4,5},{5,4},{6,7},{7,6},{8,9},{9,8},{10,11... | collective-permute-start | bytes 786440 | tf_op jit(solution)/shard_map/ppermute | solution.py:317
  25.8 2.9 %copy-start = (bf16[1024,512]{1,0:T(8,128)(2,1)S(1)}, bf16[1024,512]{1,0:T(8,128)(2,1)}, u32[]{:S(2)}) copy-start(bf16[1024,512]{1,0:T(8,128)(2,1)} %refs_1_.1) | copy-start | bytes 3145732
  25.8 9.7 %collective-permute-start.8 = (bf16[128,512]{1,0:T(8,128)(2,1)S(1)}, bf16[128,512]{1,0:T(8,128)(2,1)S(1)}, u32[]{:S(2)}, u32[]{:S(2)}) collective-permute-start(bf16[128,512]{1,0:T(8,128)(2,1)S(1)} %add_convert_fusion), channel_id=1, source_target_pairs={{0,4},{1,5},{2,6},{3,7},{4,0},{5,1},{6,2},{7,3},{8,12},{9,13},{10,... | collective-permute-start | bytes 393224 | tf_op jit(solution)/shard_map/ppermute | solution.py:317

commit v2 on v0

--- a/solution.py
+++ b/solution.py
@@ -14,6 +14,7 @@
 TILES = 4
 PIECES = 4
 WIDE = 256
+SPAN = 512
 NT = (((1,), (1,)), ((), ()))
 TN = (((0,), (0,)), ((), ()))
 VMEM = pl.BlockSpec(memory_space=pltpu.VMEM)
@@ -95,8 +96,8 @@
 
 def columns(rows):
     for half in range(2):
-        for at in range(0, rows, WIDE):
-            yield half, slice(at, at + WIDE), slice(half * rows + at, half * rows + at + WIDE)
+        for at in range(0, rows, SPAN):
+            yield half, slice(at, at + SPAN), slice(half * rows + at, half * rows + at + SPAN)
 
 
 def score_kernel(ks, temper, *refs):
@@ -115,7 +116,7 @@
         s = lax.dot_general(table, es[half][at, :], NT, preferred_element_type=F32) * temper
         cuts = [s[m * own : (m + 1) * own] for m in range(n)]
         if 0 in ks and half == 0:
-            hit = goal_ref[:, at] == lax.broadcasted_iota(jnp.int32, (own, WIDE), 0)
+            hit = goal_ref[:, at] == lax.broadcasted_iota(jnp.int32, (own, SPAN), 0)
             found = jnp.sum(jnp.where(hit, cuts[ks.index(0)], 0.0), axis=0, keepdims=True)
             refs[3 + n][:, at] = found
         top = None if st_in is None else st_in[0:1, to]

time: 36.4 us -> 36.4 us (level)
  no operation moved by 1% of the time
where the time goes in v2:
time: 36.4 us; the launch traced here: 36.3 us
  starting transfers between devices  12.3 us (34%)
  Pallas kernels  11.2 us (31%)
  waiting for transfers between devices  10.4 us (29%)
  between operations  1.46 us (4%)
  other arithmetic  0.79 us (2%)
    ppermute x13, starting transfers between devices, trade(): return lax.ppermute(x, 'vid', [(i, i ^ k) for i in range(videos)])  12.3 us
    ppermute x13, waiting for transfers between devices, trade(): return lax.ppermute(x, 'vid', [(i, i ^ k) for i in range(videos)])  10.4 us
    pallas_call x1, Pallas kernels, embed(): pl.pallas_call(embed_kernel, in_specs=[ANYWHERE, ANYWHERE], out_specs=VME...  3.18 us
    pallas_call x2, Pallas kernels, score(): pl.pallas_call(lambda *refs: score_kernel(ks, temper, *refs), in_specs=[V...  2.25 us
    pallas_call x1, Pallas kernels, back(): pl.pallas_call(lambda *refs: back_kernel(temper, *refs), in_specs=[VMEM]...  2.13 us
    pallas_call x2, Pallas kernels, share(): pl.pallas_call(lambda *refs: share_kernel(ks, *refs), in_specs=[VMEM] * (...  1.91 us
    pallas_call x2, Pallas kernels, rows_of(): pl.pallas_call(lambda *refs: rows_kernel(n, rows if theirs else 0, *refs)...  1.48 us
    mul x1, other arithmetic, shards(): return (loss[0].reshape(-1), frame_grad, sums[0] * temper)  0.76 us
  transfers between devices with their start and end apart: 13, of which 7 were waited for; matrix products, arithmetic and copies ran while one was open for 0% of the time, Pallas kernels for 27%

profile of v2, /device:TPU:0, one launch (start us, length us, event | category | flops | bytes accessed | tf_op | source)
XLA Modules:
  0.0 36.3 jit_solution(16671095011051620751)
XLA Ops:
  0.7 4.1 %collective-permute-start.1 = (bf16[128,512]{1,0:T(8,128)(2,1)}, bf16[128,512]{1,0:T(8,128)(2,1)S(1)}, u32[]{:S(2)}, u32[]{:S(2)}) collective-permute-start(bf16[128,512]{1,0:T(8,128)(2,1)} %refs_4_.5), channel_id=1, source_target_pairs={{0,4},{1,5},{2,6},{3,7},{4,0},{5,1},{6,2},{7,3},{8,12},{9,13},{10,... | collective-permute-start | bytes 393224 | tf_op jit(solution)/shard_map/ppermute | solution.py:289
  4.8 1.6 %collective-permute-start = (bf16[128,512]{1,0:T(8,128)(2,1)}, bf16[128,512]{1,0:T(8,128)(2,1)S(1)}, u32[]{:S(2)}, u32[]{:S(2)}) collective-permute-start(bf16[128,512]{1,0:T(8,128)(2,1)} %refs_4_.5), channel_id=1, source_target_pairs={{0,2},{1,3},{2,0},{3,1},{4,6},{5,7},{6,4},{7,5},{8,10},{9,11},{10,... | collective-permute-start | bytes 393224 | tf_op jit(solution)/shard_map/ppermute | solution.py:289
  6.3 3.2 %embed.1.refs_0_.refs_2_ = bf16[1024,512]{1,0:T(8,128)(2,1)S(1)} custom-call(bf16[1024,1024]{1,0:T(8,128)(2,1)} %x_hbm.1, bf16[1024,512]{1,0:T(8,128)(2,1)} %refs_1_.1), custom_call_target="tpu_custom_call" | custom-call | flops 1073741824 | bytes 4194304 | tf_op jit(solution)/shard_map/embed/pallas_call | solution.py:56
  9.5 1.9 %collective-permute-done.1.refs_5_ = bf16[128,512]{1,0:T(8,128)(2,1)S(1)} collective-permute-done((bf16[128,512]{1,0:T(8,128)(2,1)}, bf16[128,512]{1,0:T(8,128)(2,1)S(1)}, u32[]{:S(2)}, u32[]{:S(2)}) %collective-permute-start.1) | collective-permute-done | bytes 131104 | tf_op jit(solution)/shard_map/ppermute | solution.py:289
  11.4 0.2 collective-permute-done.refs_6_
  11.6 0.0 collective-permute-start.2
  11.6 1.4 %collective-permute-start.4 = (bf16[128,512]{1,0:T(8,128)(2,1)S(1)}, bf16[128,512]{1,0:T(8,128)(2,1)S(1)}, u32[]{:S(2)}, u32[]{:S(2)}) collective-permute-start(bf16[128,512]{1,0:T(8,128)(2,1)S(1)} %collective-permute-done.1.refs_5_), channel_id=1, source_target_pairs={{0,2},{1,3},{2,0},{3,1},{4,6},{5,7},{6,4},{7,5},{8,10},{9,11},{10,... | collective-permute-start | bytes 393224 | tf_op jit(solution)/shard_map/ppermute | solution.py:289
  13.7 0.3 sight.1
  14.0 0.3 collective-permute-start.3
  14.3 1.0 %collective-permute-done.3.refs_3_ = f32[4,1024]{1,0:T(4,128)S(1)} collective-permute-done((f32[4,1024]{1,0:T(4,128)S(1)}, f32[4,1024]{1,0:T(4,128)S(1)}, u32[]{:S(2)}, u32[]{:S(2)}) %collective-permute-start.3) | collective-permute-done | bytes 16416 | tf_op jit(solution)/shard_map/ppermute | solution.py:289
  15.2 0.0 collective-permute-done.2.refs_1_.refs_3_
  15.2 1.4 %score_1.1 = (f32[128,2048]{1,0:T(8,128)S(1)}, f32[128,2048]{1,0:T(8,128)S(1)}, f32[128,2048]{1,0:T(8,128)S(1)}, f32[1,2048]{1,0:T(1,128)S(1)}, f32[2,2048]{1,0:T(2,128)S(1)}, /*index=5*/f32[1,1024]{1,0:T(1,128)S(1)}) custom-call(bf16[1024,512]{1,0:T(8,128)(2,1)S(1)} %embed.1.refs_0_.refs_2_, bf16[1024,512]{1,0:T(8,128)(2,1)S(1)} %collective-permute-done.2.refs_1_.refs_3_, ...), custom_call_target="tpu_custom_call" | custom-call | flops 805306368 | bytes 5242880 | tf_op jit(solution)/shard_map/score_1/pallas_call | solution.py:145
  16.6 0.9 %collective-permute-done.4.refs_4_.refs_7_ = bf16[128,512]{1,0:T(8,128)(2,1)S(1)} collective-permute-done((bf16[128,512]{1,0:T(8,128)(2,1)S(1)}, bf16[128,512]{1,0:T(8,128)(2,1)S(1)}, u32[]{:S(2)}, u32[]{:S(2)}) %collective-permute-start.4) | collective-permute-done | bytes 131104 | tf_op jit(solution)/shard_map/ppermute | solution.py:289
  17.5 0.9 %score_3.1 = (f32[128,2048]{1,0:T(8,128)S(1)}, f32[1,2048]{1,0:T(1,128)S(1)}, f32[2,2048]{1,0:T(2,128)S(1)}) custom-call(bf16[1024,512]{1,0:T(8,128)(2,1)S(1)} %embed.1.refs_0_.refs_2_, bf16[1024,512]{1,0:T(8,128)(2,1)S(1)} %collective-permute-done.2.refs_1_.refs_3_, f32[4,1024]{1,0:T(4,128)S(1)} %get-tuple-element.36.refs_2_, ...), custom_call_target="tpu_custom_call" | custom-call | flops 268435456 | bytes 3145728 | tf_op jit(solution)/shard_map/score_3/pallas_call | solution.py:145
  18.4 0.1 collective-permute-start.5
  18.5 1.2 %collective-permute-done.5.refs_1_ = f32[2,2048]{1,0:T(2,128)S(1)} collective-permute-done((f32[2,2048]{1,0:T(2,128)S(1)}, f32[2,2048]{1,0:T(2,128)S(1)}, u32[]{:S(2)}, u32[]{:S(2)}) %collective-permute-start.5) | collective-permute-done | bytes 16416 | tf_op jit(solution)/shard_map/ppermute | solution.py:289
  19.7 0.5 %share_3.1 = (bf16[128,2048]{1,0:T(8,128)(2,1)S(1)}, bf16[128,512]{1,0:T(8,128)(2,1)S(1)}) custom-call(f32[2,2048]{1,0:T(2,128)S(1)} %get-tuple-element.42.refs_0_, f32[2,2048]{1,0:T(2,128)S(1)} %collective-permute-done.5.refs_1_, bf16[1024,512]{1,0:T(8,128)(2,1)S(1)} %embed.1.refs_0_.refs_2_, bf16[1024,512]{1,0:T(8,128)(2,1)S(1)} %collective-permute-done.2.refs_1_.refs_3_, ...), custom_call_target="tpu_custom_call" | custom-call | flops 268435456 | bytes 3670016 | tf_op jit(solution)/shard_map/share_3/pallas_call | solution.py:201
  20.1 1.5 %collective-permute-start.6 = (bf16[128,512]{1,0:T(8,128)(2,1)S(1)}, bf16[128,512]{1,0:T(8,128)(2,1)S(1)}, u32[]{:S(2)}, u32[]{:S(2)}) collective-permute-start(bf16[128,512]{1,0:T(8,128)(2,1)S(1)} %get-tuple-element.54), channel_id=1, source_target_pairs={{0,2},{1,3},{2,0},{3,1},{4,6},{5,7},{6,4},{7,5},{8,10},{9,11},{10,... | collective-permute-start | bytes 393224 | tf_op jit(solution)/shard_map/ppermute | solution.py:289
  21.6 1.5 %share_2.1 = (bf16[128,2048]{1,0:T(8,128)(2,1)S(1)}, bf16[128,2048]{1,0:T(8,128)(2,1)S(1)}, bf16[128,2048]{1,0:T(8,128)(2,1)S(1)}, f32[128,512]{1,0:T(8,128)S(1)...) custom-call(f32[2,2048]{1,0:T(2,128)S(1)} %get-tuple-element.42.refs_0_, ...), custom_call_target="tpu_custom_call" | custom-call | flops 805306368 | bytes 6815744 | tf_op jit(solution)/shard_map/share_2/pallas_call | solution.py:201
  23.1 0.7 %rows_theirs.1 = (bf16[256,512]{1,0:T(8,128)(2,1)S(1)}, bf16[256,512]{1,0:T(8,128)(2,1)S(1)}, bf16[256,512]{1,0:T(8,128)(2,1)S(1)}, bf16[256,512]{1,0:T(8,128)(2,1)S(1)}) custom-call(bf16[128,2048]{1,0:T(8,128)(2,1)S(1)} %get-tuple-element.55.refs_0_, bf16[128,2048]{1,0:T(8,128)(2,1)S(1)} %get-tuple-element.56.refs_1_, ...), custom_call_target="tpu_custom_call" | custom-call | flops 536870912 | bytes 2621440 | tf_op jit(solution)/shard_map/rows_theirs/pallas_call | solution.py:233
  23.8 0.1 collective-permute-start.8
  23.9 0.7 %collective-permute-start.12 = (bf16[128,512]{1,0:T(8,128)(2,1)S(1)}, bf16[128,512]{1,0:T(8,128)(2,1)S(1)}, u32[]{:S(2)}, u32[]{:S(2)}) collective-permute-start(bf16[128,512]{1,0:T(8,128)(2,1)S(1)} %get-tuple-element.65), channel_id=1, source_target_pairs={{0,2},{1,3},{2,0},{3,1},{4,6},{5,7},{6,4},{7,5},{8,10},{9,11},{10,... | collective-permute-start | bytes 393224 | tf_op jit(solution)/shard_map/ppermute | solution.py:289
  24.6 0.2 collective-permute-start.9
  24.7 0.3 collective-permute-start.10
  25.1 0.7 %collective-permute-done.6 = bf16[128,512]{1,0:T(8,128)(2,1)S(1)} collective-permute-done((bf16[128,512]{1,0:T(8,128)(2,1)S(1)}, bf16[128,512]{1,0:T(8,128)(2,1)S(1)}, u32[]{:S(2)}, u32[]{:S(2)}) %collective-permute-start.6) | collective-permute-done | bytes 131104 | tf_op jit(solution)/shard_map/ppermute | solution.py:289
  25.8 0.0 copy-start
  25.8 0.0 collective-permute-done.8.refs_2_
  25.8 2.1 %collective-permute-start.7 = (bf16[128,512]{1,0:T(8,128)(2,1)S(1)}, bf16[128,512]{1,0:T(8,128)(2,1)S(1)}, u32[]{:S(2)}, u32[]{:S(2)}) collective-permute-start(bf16[128,512]{1,0:T(8,128)(2,1)S(1)} %add_convert_fusion), channel_id=1, source_target_pairs={{0,4},{1,5},{2,6},{3,7},{4,0},{5,1},{6,2},{7,3},{8,12},{9,13},{10,... | collective-permute-start | bytes 393224 | tf_op jit(solution)/shard_map/ppermute | solution.py:289
  27.9 0.7 %rows_mine.1.refs_0_ = f32[1024,512]{1,0:T(8,128)S(1)} custom-call(bf16[128,2048]{1,0:T(8,128)(2,1)S(1)} %get-tuple-element.55.refs_0_, bf16[128,2048]{1,0:T(8,128)(2,1)S(1)} %get-tuple-element.56.refs_1_, bf16[128,2048]{1,0:T(8,128)(2,1)S(1)} %get-tuple-element.57.refs_2_, bf16[128,2048]{1,0:T(8,128)(2,1)S(1)} %get-tuple-element.58.refs_3_, ...), custom_call_target="tpu_custom_call" | custom-call | flops 536870912 | bytes 2621440 | tf_op jit(solution)/shard_map/rows_mine/pallas_call | solution.py:233
  28.7 2.1 %back.1 = bf16[1024,1024]{1,0:T(8,128)(2,1)} custom-call(f32[1024,512]{1,0:T(8,128)S(1)} %rows_mine.1.refs_0_, bf16[1024,512]{1,0:T(8,128)(2,1)S(1)} %copy-done, bf16[256,512]{1,0:T(8,128)(2,1)S(1)} %collective-permute-done.8.refs_2_, bf16[256,512]{1,0:T(8,128)(2,1)S(1)} %collective-permute-done.9.refs_3_, ...), custom_call_target="tpu_custom_call" | custom-call | flops 1073741824 | bytes 3145728 | tf_op jit(solution)/shard_map/back/pallas_call | solution.py:265
  30.9 4.6 %collective-permute-done.7 = bf16[128,512]{1,0:T(8,128)(2,1)S(1)} collective-permute-done((bf16[128,512]{1,0:T(8,128)(2,1)S(1)}, bf16[128,512]{1,0:T(8,128)(2,1)S(1)}, u32[]{:S(2)}, u32[]{:S(2)}) %collective-permute-start.7) | collective-permute-done | bytes 131104 | tf_op jit(solution)/shard_map/ppermute | solution.py:289
  35.5 0.8 %add_multiply_fusion = f32[128,512]{1,0:T(8,128)} fusion(bf16[128,512]{1,0:T(8,128)(2,1)S(1)} %collective-permute-done.7, f32[128,512]{1,0:T(8,128)S(1)} %get-tuple-element.64, bf16[128,512]{1,0:T(8,128)(2,1)S(1)} %collective-permute-done.12), kind=kLoop, calls=%fused_computation | loop fusion | flops 327680 | bytes 786432 | tf_op jit(solution)/shard_map/mul | solution.py:339
  (15 shorter events, 0.1 us)
Async XLA Ops:
  0.6 14.6 %copy-start.1 = (bf16[128,512]{1,0:T(8,128)(2,1)S(1)}, bf16[128,512]{1,0:T(8,128)(2,1)}, u32[]{:S(2)}) copy-start(bf16[128,512]{1,0:T(8,128)(2,1)} %refs_4_.5) | copy-start | bytes 393220
  0.6 13.1 %copy-start.4 = (s32[1,64]{1,0:T(1,128)S(1)}, s32[1,64]{1,0:T(1,128)}, u32[]{:S(2)}) copy-start(s32[1,64]{1,0:T(1,128)} %ts_ref.1) | copy-start | bytes 772
  0.7 13.1 %copy-start.3 = (s32[1,64]{1,0:T(1,128)S(1)}, s32[1,64]{1,0:T(1,128)}, u32[]{:S(2)}) copy-start(s32[1,64]{1,0:T(1,128)} %tf_ref.1) | copy-start | bytes 772
  0.7 14.6 %copy-start.2 = (s32[1024]{0:T(1024)S(1)}, s32[1024]{0:T(1024)}, u32[]{:S(2)}) copy-start(s32[1024]{0:T(1024)} %param.10) | copy-start | bytes 12292
  0.7 10.7 %collective-permute-start.1 = (bf16[128,512]{1,0:T(8,128)(2,1)}, bf16[128,512]{1,0:T(8,128)(2,1)S(1)}, u32[]{:S(2)}, u32[]{:S(2)}) collective-permute-start(bf16[128,512]{1,0:T(8,128)(2,1)} %refs_4_.5), channel_id=1, source_target_pairs={{0,4},{1,5},{2,6},{3,7},{4,0},{5,1},{6,2},{7,3},{8,12},{9,13},{10,... | collective-permute-start | bytes 393224 | tf_op jit(solution)/shard_map/ppermute | solution.py:289
  4.8 6.8 %collective-permute-start = (bf16[128,512]{1,0:T(8,128)(2,1)}, bf16[128,512]{1,0:T(8,128)(2,1)S(1)}, u32[]{:S(2)}, u32[]{:S(2)}) collective-permute-start(bf16[128,512]{1,0:T(8,128)(2,1)} %refs_4_.5), channel_id=1, source_target_pairs={{0,2},{1,3},{2,0},{3,1},{4,6},{5,7},{6,4},{7,5},{8,10},{9,11},{10,... | collective-permute-start | bytes 393224 | tf_op jit(solution)/shard_map/ppermute | solution.py:289
  11.6 3.6 %collective-permute-start.2 = (bf16[1024,512]{1,0:T(8,128)(2,1)S(1)}, bf16[1024,512]{1,0:T(8,128)(2,1)S(1)}, u32[]{:S(2)}, u32[]{:S(2)}) collective-permute-start(bf16[1024,512]{1,0:T(8,128)(2,1)S(1)} %embed.1.refs_0_.refs_2_), channel_id=1, source_target_pairs={{0,1},{1,0},{2,3},{3,2},{4,5},{5,4},{6,7},{7,6},{8,9},{9,8},{10,11... | collective-permute-start | bytes 3145736 | tf_op jit(solution)/shard_map/ppermute | solution.py:289
  11.6 5.9 %collective-permute-start.4 = (bf16[128,512]{1,0:T(8,128)(2,1)S(1)}, bf16[128,512]{1,0:T(8,128)(2,1)S(1)}, u32[]{:S(2)}, u32[]{:S(2)}) collective-permute-start(bf16[128,512]{1,0:T(8,128)(2,1)S(1)} %collective-permute-done.1.refs_5_), channel_id=1, source_target_pairs={{0,2},{1,3},{2,0},{3,1},{4,6},{5,7},{6,4},{7,5},{8,10},{9,11},{10,... | collective-permute-start | bytes 393224 | tf_op jit(solution)/shard_map/ppermute | solution.py:289
  14.0 1.2 %collective-permute-start.3 = (f32[4,1024]{1,0:T(4,128)S(1)}, f32[4,1024]{1,0:T(4,128)S(1)}, u32[]{:S(2)}, u32[]{:S(2)}) collective-permute-start(f32[4,1024]{1,0:T(4,128)S(1)} %get-tuple-element.37), channel_id=1, source_target_pairs={{0,1},{1,0},{2,3},{3,2},{4,5},{5,4},{6,7},{7,6},{8,9},{9,8},{10,11... | collective-permute-start | bytes 49160 | tf_op jit(solution)/shard_map/ppermute | solution.py:289
  18.4 1.2 %collective-permute-start.5 = (f32[2,2048]{1,0:T(2,128)S(1)}, f32[2,2048]{1,0:T(2,128)S(1)}, u32[]{:S(2)}, u32[]{:S(2)}) collective-permute-start(f32[2,2048]{1,0:T(2,128)S(1)} %get-tuple-element.42.refs_0_), channel_id=1, source_target_pairs={{0,1},{1,0},{2,3},{3,2},{4,5},{5,4},{6,7},{7,6},{8,9},{9,8},{10,11... | collective-permute-start | bytes 49160 | tf_op jit(solution)/shard_map/ppermute | solution.py:289
  20.1 5.6 %collective-permute-start.6 = (bf16[128,512]{1,0:T(8,128)(2,1)S(1)}, bf16[128,512]{1,0:T(8,128)(2,1)S(1)}, u32[]{:S(2)}, u32[]{:S(2)}) collective-permute-start(bf16[128,512]{1,0:T(8,128)(2,1)S(1)} %get-tuple-element.54), channel_id=1, source_target_pairs={{0,2},{1,3},{2,0},{3,1},{4,6},{5,7},{6,4},{7,5},{8,10},{9,11},{10,... | collective-permute-start | bytes 393224 | tf_op jit(solution)/shard_map/ppermute | solution.py:289
  23.8 2.0 %collective-permute-start.8 = (bf16[256,512]{1,0:T(8,128)(2,1)S(1)}, bf16[256,512]{1,0:T(8,128)(2,1)S(1)}, u32[]{:S(2)}, u32[]{:S(2)}) collective-permute-start(bf16[256,512]{1,0:T(8,128)(2,1)S(1)} %get-tuple-element.59), channel_id=1, source_target_pairs={{0,1},{1,0},{2,3},{3,2},{4,5},{5,4},{6,7},{7,6},{8,9},{9,8},{10,11... | collective-permute-start | bytes 786440 | tf_op jit(solution)/shard_map/ppermute | solution.py:289
  23.9 11.6 %collective-permute-start.12 = (bf16[128,512]{1,0:T(8,128)(2,1)S(1)}, bf16[128,512]{1,0:T(8,128)(2,1)S(1)}, u32[]{:S(2)}, u32[]{:S(2)}) collective-permute-start(bf16[128,512]{1,0:T(8,128)(2,1)S(1)} %get-tuple-element.65), channel_id=1, source_target_pairs={{0,2},{1,3},{2,0},{3,1},{4,6},{5,7},{6,4},{7,5},{8,10},{9,11},{10,... | collective-permute-start | bytes 393224 | tf_op jit(solution)/shard_map/ppermute | solution.py:289
  24.6 4.1 %collective-permute-start.9 = (bf16[256,512]{1,0:T(8,128)(2,1)S(1)}, bf16[256,512]{1,0:T(8,128)(2,1)S(1)}, u32[]{:S(2)}, u32[]{:S(2)}) collective-permute-start(bf16[256,512]{1,0:T(8,128)(2,1)S(1)} %get-tuple-element.60), channel_id=1, source_target_pairs={{0,1},{1,0},{2,3},{3,2},{4,5},{5,4},{6,7},{7,6},{8,9},{9,8},{10,11... | collective-permute-start | bytes 786440 | tf_op jit(solution)/shard_map/ppermute | solution.py:289
  24.7 4.0 %collective-permute-start.10 = (bf16[256,512]{1,0:T(8,128)(2,1)S(1)}, bf16[256,512]{1,0:T(8,128)(2,1)S(1)}, u32[]{:S(2)}, u32[]{:S(2)}) collective-permute-start(bf16[256,512]{1,0:T(8,128)(2,1)S(1)} %get-tuple-element.61), channel_id=1, source_target_pairs={{0,1},{1,0},{2,3},{3,2},{4,5},{5,4},{6,7},{7,6},{8,9},{9,8},{10,11... | collective-permute-start | bytes 786440 | tf_op jit(solution)/shard_map/ppermute | solution.py:289
  25.7 3.0 %collective-permute-start.11 = (bf16[256,512]{1,0:T(8,128)(2,1)S(1)}, bf16[256,512]{1,0:T(8,128)(2,1)S(1)}, u32[]{:S(2)}, u32[]{:S(2)}) collective-permute-start(bf16[256,512]{1,0:T(8,128)(2,1)S(1)} %get-tuple-element.62), channel_id=1, source_target_pairs={{0,1},{1,0},{2,3},{3,2},{4,5},{5,4},{6,7},{7,6},{8,9},{9,8},{10,11... | collective-permute-start | bytes 786440 | tf_op jit(solution)/shard_map/ppermute | solution.py:289
  25.8 2.9 %copy-start = (bf16[1024,512]{1,0:T(8,128)(2,1)S(1)}, bf16[1024,512]{1,0:T(8,128)(2,1)}, u32[]{:S(2)}) copy-start(bf16[1024,512]{1,0:T(8,128)(2,1)} %refs_1_.1) | copy-start | bytes 3145732
  25.8 9.7 %collective-permute-start.7 = (bf16[128,512]{1,0:T(8,128)(2,1)S(1)}, bf16[128,512]{1,0:T(8,128)(2,1)S(1)}, u32[]{:S(2)}, u32[]{:S(2)}) collective-permute-start(bf16[128,512]{1,0:T(8,128)(2,1)S(1)} %add_convert_fusion), channel_id=1, source_target_pairs={{0,4},{1,5},{2,6},{3,7},{4,0},{5,1},{6,2},{7,3},{8,12},{9,13},{10,... | collective-permute-start | bytes 393224 | tf_op jit(solution)/shard_map/ppermute | solution.py:289

commit v3 on v0

--- a/solution.py
+++ b/solution.py
@@ -326,6 +326,7 @@
     parts = [qs[k] for k in order], [mine[k] for k in order]
     lent = [trade(piece, 1) for piece in rows_of(*parts, True)]
     (own_rows,) = rows_of(*parts, False)
+    sums[1], lent[0] = lax.optimization_barrier((sums[1], lent[0]))
     frame_grad = back(own_rows, lent, w_frame, temper)
     bit = 1
     while bit < chips:

time: 36.4 us -> 35.3 us (0.970)
  waiting for transfers between devices: 10.4 us -> 7.77 us
  starting transfers between devices: 12.3 us -> 13.9 us
    ppermute x13, waiting for transfers between devices: 10.4 us -> 7.77 us  [trade(): return lax.ppermute(x, 'vid', [(i, i ^ k) for i in range(videos)])]
    ppermute x13, starting transfers between devices: 12.3 us -> 13.9 us  [trade(): return lax.ppermute(x, 'vid', [(i, i ^ k) for i in range(videos)])]
  transfers between devices with their start and end apart: 13 -> 13, of which waited for: 7 -> 8; matrix products, arithmetic and copies ran while one was open for 0% -> 0% of each run, Pallas kernels for 27% -> 28%
where the time goes in v3:
time: 35.3 us; the launch traced here: 35.2 us
  starting transfers between devices  13.9 us (39%)
  Pallas kernels  11.2 us (32%)
  waiting for transfers between devices  7.77 us (22%)
  between operations  1.44 us (4%)
  other arithmetic  0.78 us (2%)
    ppermute x13, starting transfers between devices, trade(): return lax.ppermute(x, 'vid', [(i, i ^ k) for i in range(videos)])  13.9 us
    ppermute x13, waiting for transfers between devices, trade(): return lax.ppermute(x, 'vid', [(i, i ^ k) for i in range(videos)])  7.77 us
    pallas_call x1, Pallas kernels, embed(): pl.pallas_call(embed_kernel, in_specs=[ANYWHERE, ANYWHERE], out_specs=VME...  3.18 us
    pallas_call x2, Pallas kernels, score(): pl.pallas_call(lambda *refs: score_kernel(ks, temper, *refs), in_specs=[V...  2.26 us
    pallas_call x1, Pallas kernels, back(): pl.pallas_call(lambda *refs: back_kernel(temper, *refs), in_specs=[VMEM]...  2.13 us
    pallas_call x2, Pallas kernels, share(): pl.pallas_call(lambda *refs: share_kernel(ks, *refs), in_specs=[VMEM] * (...  1.9 us
    pallas_call x2, Pallas kernels, rows_of(): pl.pallas_call(lambda *refs: rows_kernel(n, rows if theirs else 0, *refs)...  1.49 us
    mul x1, other arithmetic, shards(): return (loss[0].reshape(-1), frame_grad, sums[0] * temper)  0.75 us
  transfers between devices with their start and end apart: 13, of which 8 were waited for; matrix products, arithmetic and copies ran while one was open for 0% of the time, Pallas kernels for 28%

profile of v3, /device:TPU:0, one launch (start us, length us, event | category | flops | bytes accessed | tf_op | source)
XLA Modules:
  0.0 35.2 jit_solution(11793284972468352570)
XLA Ops:
  0.7 4.1 %collective-permute-start.1 = (bf16[128,512]{1,0:T(8,128)(2,1)}, bf16[128,512]{1,0:T(8,128)(2,1)S(1)}, u32[]{:S(2)}, u32[]{:S(2)}) collective-permute-start(bf16[128,512]{1,0:T(8,128)(2,1)} %refs_4_.5), channel_id=1, source_target_pairs={{0,4},{1,5},{2,6},{3,7},{4,0},{5,1},{6,2},{7,3},{8,12},{9,13},{10,... | collective-permute-start | bytes 393224 | tf_op jit(solution)/shard_map/ppermute | solution.py:288
  4.8 1.6 %collective-permute-start = (bf16[128,512]{1,0:T(8,128)(2,1)}, bf16[128,512]{1,0:T(8,128)(2,1)S(1)}, u32[]{:S(2)}, u32[]{:S(2)}) collective-permute-start(bf16[128,512]{1,0:T(8,128)(2,1)} %refs_4_.5), channel_id=1, source_target_pairs={{0,2},{1,3},{2,0},{3,1},{4,6},{5,7},{6,4},{7,5},{8,10},{9,11},{10,... | collective-permute-start | bytes 393224 | tf_op jit(solution)/shard_map/ppermute | solution.py:288
  6.3 3.2 %embed.1.refs_0_.refs_2_ = bf16[1024,512]{1,0:T(8,128)(2,1)S(1)} custom-call(bf16[1024,1024]{1,0:T(8,128)(2,1)} %x_hbm.1, bf16[1024,512]{1,0:T(8,128)(2,1)} %refs_1_.1), custom_call_target="tpu_custom_call" | custom-call | flops 1073741824 | bytes 4194304 | tf_op jit(solution)/shard_map/embed/pallas_call | solution.py:55
  9.5 1.9 %collective-permute-done.1.refs_5_ = bf16[128,512]{1,0:T(8,128)(2,1)S(1)} collective-permute-done((bf16[128,512]{1,0:T(8,128)(2,1)}, bf16[128,512]{1,0:T(8,128)(2,1)S(1)}, u32[]{:S(2)}, u32[]{:S(2)}) %collective-permute-start.1) | collective-permute-done | bytes 131104 | tf_op jit(solution)/shard_map/ppermute | solution.py:288
  11.4 0.2 collective-permute-done.refs_6_
  11.6 1.4 %collective-permute-start.4 = (bf16[128,512]{1,0:T(8,128)(2,1)S(1)}, bf16[128,512]{1,0:T(8,128)(2,1)S(1)}, u32[]{:S(2)}, u32[]{:S(2)}) collective-permute-start(bf16[128,512]{1,0:T(8,128)(2,1)S(1)} %collective-permute-done.1.refs_5_), channel_id=1, source_target_pairs={{0,2},{1,3},{2,0},{3,1},{4,6},{5,7},{6,4},{7,5},{8,10},{9,11},{10,... | collective-permute-start | bytes 393224 | tf_op jit(solution)/shard_map/ppermute | solution.py:288
  13.7 0.3 sight.1
  14.0 0.3 collective-permute-start.3
  14.3 1.0 %collective-permute-done.3.refs_3_ = f32[4,1024]{1,0:T(4,128)S(1)} collective-permute-done((f32[4,1024]{1,0:T(4,128)S(1)}, f32[4,1024]{1,0:T(4,128)S(1)}, u32[]{:S(2)}, u32[]{:S(2)}) %collective-permute-start.3) | collective-permute-done | bytes 16416 | tf_op jit(solution)/shard_map/ppermute | solution.py:288
  15.2 1.4 %score_1.1 = (f32[128,2048]{1,0:T(8,128)S(1)}, f32[128,2048]{1,0:T(8,128)S(1)}, f32[128,2048]{1,0:T(8,128)S(1)}, f32[1,2048]{1,0:T(1,128)S(1)}, f32[2,2048]{1,0:T(2,128)S(1)}, /*index=5*/f32[1,1024]{1,0:T(1,128)S(1)}) custom-call(bf16[1024,512]{1,0:T(8,128)(2,1)S(1)} %embed.1.refs_0_.refs_2_, bf16[1024,512]{1,0:T(8,128)(2,1)S(1)} %collective-permute-done.2.refs_1_.refs_3_, ...), custom_call_target="tpu_custom_call" | custom-call | flops 805306368 | bytes 5242880 | tf_op jit(solution)/shard_map/score_1/pallas_call | solution.py:144
  16.6 0.9 %collective-permute-done.4.refs_4_.refs_7_ = bf16[128,512]{1,0:T(8,128)(2,1)S(1)} collective-permute-done((bf16[128,512]{1,0:T(8,128)(2,1)S(1)}, bf16[128,512]{1,0:T(8,128)(2,1)S(1)}, u32[]{:S(2)}, u32[]{:S(2)}) %collective-permute-start.4) | collective-permute-done | bytes 131104 | tf_op jit(solution)/shard_map/ppermute | solution.py:288
  17.5 0.9 %score_3.1 = (f32[128,2048]{1,0:T(8,128)S(1)}, f32[1,2048]{1,0:T(1,128)S(1)}, f32[2,2048]{1,0:T(2,128)S(1)}) custom-call(bf16[1024,512]{1,0:T(8,128)(2,1)S(1)} %embed.1.refs_0_.refs_2_, bf16[1024,512]{1,0:T(8,128)(2,1)S(1)} %collective-permute-done.2.refs_1_.refs_3_, f32[4,1024]{1,0:T(4,128)S(1)} %get-tuple-element.38.refs_2_, ...), custom_call_target="tpu_custom_call" | custom-call | flops 268435456 | bytes 3145728 | tf_op jit(solution)/shard_map/score_3/pallas_call | solution.py:144
  18.4 0.1 collective-permute-start.5
  18.5 1.2 %collective-permute-done.5.refs_1_ = f32[2,2048]{1,0:T(2,128)S(1)} collective-permute-done((f32[2,2048]{1,0:T(2,128)S(1)}, f32[2,2048]{1,0:T(2,128)S(1)}, u32[]{:S(2)}, u32[]{:S(2)}) %collective-permute-start.5) | collective-permute-done | bytes 16416 | tf_op jit(solution)/shard_map/ppermute | solution.py:288
  19.6 0.4 %share_3.1 = (bf16[128,2048]{1,0:T(8,128)(2,1)S(1)}, bf16[128,512]{1,0:T(8,128)(2,1)S(1)}) custom-call(f32[2,2048]{1,0:T(2,128)S(1)} %get-tuple-element.44.refs_0_, f32[2,2048]{1,0:T(2,128)S(1)} %collective-permute-done.5.refs_1_, bf16[1024,512]{1,0:T(8,128)(2,1)S(1)} %embed.1.refs_0_.refs_2_, bf16[1024,512]{1,0:T(8,128)(2,1)S(1)} %collective-permute-done.2.refs_1_.refs_3_, ...), custom_call_target="tpu_custom_call" | custom-call | flops 268435456 | bytes 3670016 | tf_op jit(solution)/shard_map/share_3/pallas_call | solution.py:200
  20.1 1.5 %collective-permute-start.6 = (bf16[128,512]{1,0:T(8,128)(2,1)S(1)}, bf16[128,512]{1,0:T(8,128)(2,1)S(1)}, u32[]{:S(2)}, u32[]{:S(2)}) collective-permute-start(bf16[128,512]{1,0:T(8,128)(2,1)S(1)} %get-tuple-element.56), channel_id=1, source_target_pairs={{0,2},{1,3},{2,0},{3,1},{4,6},{5,7},{6,4},{7,5},{8,10},{9,11},{10,... | collective-permute-start | bytes 393224 | tf_op jit(solution)/shard_map/ppermute | solution.py:288
  21.6 1.5 %share_2.1 = (bf16[128,2048]{1,0:T(8,128)(2,1)S(1)}, bf16[128,2048]{1,0:T(8,128)(2,1)S(1)}, bf16[128,2048]{1,0:T(8,128)(2,1)S(1)}, f32[128,512]{1,0:T(8,128)S(1)...) custom-call(f32[2,2048]{1,0:T(2,128)S(1)} %get-tuple-element.44.refs_0_, ...), custom_call_target="tpu_custom_call" | custom-call | flops 805306368 | bytes 6815744 | tf_op jit(solution)/shard_map/share_2/pallas_call | solution.py:200
  23.1 0.7 %rows_theirs.1 = (bf16[256,512]{1,0:T(8,128)(2,1)S(1)}, bf16[256,512]{1,0:T(8,128)(2,1)S(1)}, bf16[256,512]{1,0:T(8,128)(2,1)S(1)}, bf16[256,512]{1,0:T(8,128)(2,1)S(1)}) custom-call(bf16[128,2048]{1,0:T(8,128)(2,1)S(1)} %get-tuple-element.57.refs_0_, bf16[128,2048]{1,0:T(8,128)(2,1)S(1)} %get-tuple-element.58.refs_1_, ...), custom_call_target="tpu_custom_call" | custom-call | flops 536870912 | bytes 2621440 | tf_op jit(solution)/shard_map/rows_theirs/pallas_call | solution.py:232
  23.8 0.1 collective-permute-start.8
  23.9 0.5 %collective-permute-start.9 = (bf16[256,512]{1,0:T(8,128)(2,1)S(1)}, bf16[256,512]{1,0:T(8,128)(2,1)S(1)}, u32[]{:S(2)}, u32[]{:S(2)}) collective-permute-start(bf16[256,512]{1,0:T(8,128)(2,1)S(1)} %get-tuple-element.64), channel_id=1, source_target_pairs={{0,1},{1,0},{2,3},{3,2},{4,5},{5,4},{6,7},{7,6},{8,9},{9,8},{10,11... | collective-permute-start | bytes 786440 | tf_op jit(solution)/shard_map/ppermute | solution.py:288
  24.4 0.1 collective-permute-start.10
  24.5 0.4 %collective-permute-start.11 = (bf16[256,512]{1,0:T(8,128)(2,1)S(1)}, bf16[256,512]{1,0:T(8,128)(2,1)S(1)}, u32[]{:S(2)}, u32[]{:S(2)}) collective-permute-start(bf16[256,512]{1,0:T(8,128)(2,1)S(1)} %get-tuple-element.66), channel_id=1, source_target_pairs={{0,1},{1,0},{2,3},{3,2},{4,5},{5,4},{6,7},{7,6},{8,9},{9,8},{10,11... | collective-permute-start | bytes 786440 | tf_op jit(solution)/shard_map/ppermute | solution.py:288
  24.9 0.8 %collective-permute-done.6 = bf16[128,512]{1,0:T(8,128)(2,1)S(1)} collective-permute-done((bf16[128,512]{1,0:T(8,128)(2,1)S(1)}, bf16[128,512]{1,0:T(8,128)(2,1)S(1)}, u32[]{:S(2)}, u32[]{:S(2)}) %collective-permute-start.6) | collective-permute-done | bytes 131104 | tf_op jit(solution)/shard_map/ppermute | solution.py:288
  25.8 2.1 %collective-permute-start.7 = (bf16[128,512]{1,0:T(8,128)(2,1)S(1)}, bf16[128,512]{1,0:T(8,128)(2,1)S(1)}, u32[]{:S(2)}, u32[]{:S(2)}) collective-permute-start(bf16[128,512]{1,0:T(8,128)(2,1)S(1)} %add_convert_fusion), channel_id=1, source_target_pairs={{0,4},{1,5},{2,6},{3,7},{4,0},{5,1},{6,2},{7,3},{8,12},{9,13},{10,... | collective-permute-start | bytes 393224 | tf_op jit(solution)/shard_map/ppermute | solution.py:288
  27.9 0.0 collective-permute-done.8.refs_2_
  27.9 1.7 %collective-permute-start.12 = (bf16[128,512]{1,0:T(8,128)(2,1)S(1)}, bf16[128,512]{1,0:T(8,128)(2,1)S(1)}, u32[]{:S(2)}, u32[]{:S(2)}) collective-permute-start(bf16[128,512]{1,0:T(8,128)(2,1)S(1)} %get-tuple-element.69), channel_id=1, source_target_pairs={{0,2},{1,3},{2,0},{3,1},{4,6},{5,7},{6,4},{7,5},{8,10},{9,11},{10,... | collective-permute-start | bytes 393224 | tf_op jit(solution)/shard_map/ppermute | solution.py:288
  29.6 0.7 %rows_mine.1.refs_0_ = f32[1024,512]{1,0:T(8,128)S(1)} custom-call(bf16[128,2048]{1,0:T(8,128)(2,1)S(1)} %get-tuple-element.57.refs_0_, bf16[128,2048]{1,0:T(8,128)(2,1)S(1)} %get-tuple-element.58.refs_1_, bf16[128,2048]{1,0:T(8,128)(2,1)S(1)} %get-tuple-element.59.refs_2_, bf16[128,2048]{1,0:T(8,128)(2,1)S(1)} %get-tuple-element.60.refs_3_, ...), custom_call_target="tpu_custom_call" | custom-call | flops 536870912 | bytes 2621440 | tf_op jit(solution)/shard_map/rows_mine/pallas_call | solution.py:232
  30.4 0.0 collective-permute-done.10.refs_4_
  30.4 2.1 %back.1 = bf16[1024,1024]{1,0:T(8,128)(2,1)} custom-call(f32[1024,512]{1,0:T(8,128)S(1)} %rows_mine.1.refs_0_, bf16[1024,512]{1,0:T(8,128)(2,1)S(1)} %copy-done, bf16[256,512]{1,0:T(8,128)(2,1)S(1)} %collective-permute-done.8.refs_2_, bf16[256,512]{1,0:T(8,128)(2,1)S(1)} %collective-permute-done.9.refs_3_, ...), custom_call_target="tpu_custom_call" | custom-call | flops 1073741824 | bytes 3145728 | tf_op jit(solution)/shard_map/back/pallas_call | solution.py:264
  32.6 1.8 %collective-permute-done.7 = bf16[128,512]{1,0:T(8,128)(2,1)S(1)} collective-permute-done((bf16[128,512]{1,0:T(8,128)(2,1)S(1)}, bf16[128,512]{1,0:T(8,128)(2,1)S(1)}, u32[]{:S(2)}, u32[]{:S(2)}) %collective-permute-start.7) | collective-permute-done | bytes 131104 | tf_op jit(solution)/shard_map/ppermute | solution.py:288
  34.3 0.1 collective-permute-done.12
  34.4 0.8 %add_multiply_fusion = f32[128,512]{1,0:T(8,128)} fusion(bf16[128,512]{1,0:T(8,128)(2,1)S(1)} %collective-permute-done.7, f32[128,512]{1,0:T(8,128)S(1)} %get-tuple-element.68, bf16[128,512]{1,0:T(8,128)(2,1)S(1)} %collective-permute-done.12), kind=kLoop, calls=%fused_computation | loop fusion | flops 327680 | bytes 786432 | tf_op jit(solution)/shard_map/mul | solution.py:339
  (15 shorter events, 0.1 us)
Async XLA Ops:
  0.6 14.6 %copy-start.1 = (bf16[128,512]{1,0:T(8,128)(2,1)S(1)}, bf16[128,512]{1,0:T(8,128)(2,1)}, u32[]{:S(2)}) copy-start(bf16[128,512]{1,0:T(8,128)(2,1)} %refs_4_.5) | copy-start | bytes 393220
  0.6 13.1 %copy-start.4 = (s32[1,64]{1,0:T(1,128)S(1)}, s32[1,64]{1,0:T(1,128)}, u32[]{:S(2)}) copy-start(s32[1,64]{1,0:T(1,128)} %ts_ref.1) | copy-start | bytes 772
  0.7 13.1 %copy-start.3 = (s32[1,64]{1,0:T(1,128)S(1)}, s32[1,64]{1,0:T(1,128)}, u32[]{:S(2)}) copy-start(s32[1,64]{1,0:T(1,128)} %tf_ref.1) | copy-start | bytes 772
  0.7 14.6 %copy-start.2 = (s32[1024]{0:T(1024)S(1)}, s32[1024]{0:T(1024)}, u32[]{:S(2)}) copy-start(s32[1024]{0:T(1024)} %param.10) | copy-start | bytes 12292
  0.7 10.7 %collective-permute-start.1 = (bf16[128,512]{1,0:T(8,128)(2,1)}, bf16[128,512]{1,0:T(8,128)(2,1)S(1)}, u32[]{:S(2)}, u32[]{:S(2)}) collective-permute-start(bf16[128,512]{1,0:T(8,128)(2,1)} %refs_4_.5), channel_id=1, source_target_pairs={{0,4},{1,5},{2,6},{3,7},{4,0},{5,1},{6,2},{7,3},{8,12},{9,13},{10,... | collective-permute-start | bytes 393224 | tf_op jit(solution)/shard_map/ppermute | solution.py:288
  4.8 6.8 %collective-permute-start = (bf16[128,512]{1,0:T(8,128)(2,1)}, bf16[128,512]{1,0:T(8,128)(2,1)S(1)}, u32[]{:S(2)}, u32[]{:S(2)}) collective-permute-start(bf16[128,512]{1,0:T(8,128)(2,1)} %refs_4_.5), channel_id=1, source_target_pairs={{0,2},{1,3},{2,0},{3,1},{4,6},{5,7},{6,4},{7,5},{8,10},{9,11},{10,... | collective-permute-start | bytes 393224 | tf_op jit(solution)/shard_map/ppermute | solution.py:288
  11.6 3.6 %collective-permute-start.2 = (bf16[1024,512]{1,0:T(8,128)(2,1)S(1)}, bf16[1024,512]{1,0:T(8,128)(2,1)S(1)}, u32[]{:S(2)}, u32[]{:S(2)}) collective-permute-start(bf16[1024,512]{1,0:T(8,128)(2,1)S(1)} %embed.1.refs_0_.refs_2_), channel_id=1, source_target_pairs={{0,1},{1,0},{2,3},{3,2},{4,5},{5,4},{6,7},{7,6},{8,9},{9,8},{10,11... | collective-permute-start | bytes 3145736 | tf_op jit(solution)/shard_map/ppermute | solution.py:288
  11.6 5.9 %collective-permute-start.4 = (bf16[128,512]{1,0:T(8,128)(2,1)S(1)}, bf16[128,512]{1,0:T(8,128)(2,1)S(1)}, u32[]{:S(2)}, u32[]{:S(2)}) collective-permute-start(bf16[128,512]{1,0:T(8,128)(2,1)S(1)} %collective-permute-done.1.refs_5_), channel_id=1, source_target_pairs={{0,2},{1,3},{2,0},{3,1},{4,6},{5,7},{6,4},{7,5},{8,10},{9,11},{10,... | collective-permute-start | bytes 393224 | tf_op jit(solution)/shard_map/ppermute | solution.py:288
  14.0 1.2 %collective-permute-start.3 = (f32[4,1024]{1,0:T(4,128)S(1)}, f32[4,1024]{1,0:T(4,128)S(1)}, u32[]{:S(2)}, u32[]{:S(2)}) collective-permute-start(f32[4,1024]{1,0:T(4,128)S(1)} %get-tuple-element.39), channel_id=1, source_target_pairs={{0,1},{1,0},{2,3},{3,2},{4,5},{5,4},{6,7},{7,6},{8,9},{9,8},{10,11... | collective-permute-start | bytes 49160 | tf_op jit(solution)/shard_map/ppermute | solution.py:288
  18.4 1.2 %collective-permute-start.5 = (f32[2,2048]{1,0:T(2,128)S(1)}, f32[2,2048]{1,0:T(2,128)S(1)}, u32[]{:S(2)}, u32[]{:S(2)}) collective-permute-start(f32[2,2048]{1,0:T(2,128)S(1)} %get-tuple-element.44.refs_0_), channel_id=1, source_target_pairs={{0,1},{1,0},{2,3},{3,2},{4,5},{5,4},{6,7},{7,6},{8,9},{9,8},{10,11... | collective-permute-start | bytes 49160 | tf_op jit(solution)/shard_map/ppermute | solution.py:288
  20.1 5.6 %collective-permute-start.6 = (bf16[128,512]{1,0:T(8,128)(2,1)S(1)}, bf16[128,512]{1,0:T(8,128)(2,1)S(1)}, u32[]{:S(2)}, u32[]{:S(2)}) collective-permute-start(bf16[128,512]{1,0:T(8,128)(2,1)S(1)} %get-tuple-element.56), channel_id=1, source_target_pairs={{0,2},{1,3},{2,0},{3,1},{4,6},{5,7},{6,4},{7,5},{8,10},{9,11},{10,... | collective-permute-start | bytes 393224 | tf_op jit(solution)/shard_map/ppermute | solution.py:288
  23.8 4.1 %collective-permute-start.8 = (bf16[256,512]{1,0:T(8,128)(2,1)S(1)}, bf16[256,512]{1,0:T(8,128)(2,1)S(1)}, u32[]{:S(2)}, u32[]{:S(2)}) collective-permute-start(bf16[256,512]{1,0:T(8,128)(2,1)S(1)} %get-tuple-element.62), channel_id=1, source_target_pairs={{0,1},{1,0},{2,3},{3,2},{4,5},{5,4},{6,7},{7,6},{8,9},{9,8},{10,11... | collective-permute-start | bytes 786440 | tf_op jit(solution)/shard_map/ppermute | solution.py:288
  23.9 6.5 %collective-permute-start.9 = (bf16[256,512]{1,0:T(8,128)(2,1)S(1)}, bf16[256,512]{1,0:T(8,128)(2,1)S(1)}, u32[]{:S(2)}, u32[]{:S(2)}) collective-permute-start(bf16[256,512]{1,0:T(8,128)(2,1)S(1)} %get-tuple-element.64), channel_id=1, source_target_pairs={{0,1},{1,0},{2,3},{3,2},{4,5},{5,4},{6,7},{7,6},{8,9},{9,8},{10,11... | collective-permute-start | bytes 786440 | tf_op jit(solution)/shard_map/ppermute | solution.py:288
  24.4 6.0 %collective-permute-start.10 = (bf16[256,512]{1,0:T(8,128)(2,1)S(1)}, bf16[256,512]{1,0:T(8,128)(2,1)S(1)}, u32[]{:S(2)}, u32[]{:S(2)}) collective-permute-start(bf16[256,512]{1,0:T(8,128)(2,1)S(1)} %get-tuple-element.65), channel_id=1, source_target_pairs={{0,1},{1,0},{2,3},{3,2},{4,5},{5,4},{6,7},{7,6},{8,9},{9,8},{10,11... | collective-permute-start | bytes 786440 | tf_op jit(solution)/shard_map/ppermute | solution.py:288
  24.5 5.9 %collective-permute-start.11 = (bf16[256,512]{1,0:T(8,128)(2,1)S(1)}, bf16[256,512]{1,0:T(8,128)(2,1)S(1)}, u32[]{:S(2)}, u32[]{:S(2)}) collective-permute-start(bf16[256,512]{1,0:T(8,128)(2,1)S(1)} %get-tuple-element.66), channel_id=1, source_target_pairs={{0,1},{1,0},{2,3},{3,2},{4,5},{5,4},{6,7},{7,6},{8,9},{9,8},{10,11... | collective-permute-start | bytes 786440 | tf_op jit(solution)/shard_map/ppermute | solution.py:288
  25.8 8.6 %collective-permute-start.7 = (bf16[128,512]{1,0:T(8,128)(2,1)S(1)}, bf16[128,512]{1,0:T(8,128)(2,1)S(1)}, u32[]{:S(2)}, u32[]{:S(2)}) collective-permute-start(bf16[128,512]{1,0:T(8,128)(2,1)S(1)} %add_convert_fusion), channel_id=1, source_target_pairs={{0,4},{1,5},{2,6},{3,7},{4,0},{5,1},{6,2},{7,3},{8,12},{9,13},{10,... | collective-permute-start | bytes 393224 | tf_op jit(solution)/shard_map/ppermute | solution.py:288
  27.9 2.5 %copy-start = (bf16[1024,512]{1,0:T(8,128)(2,1)S(1)}, bf16[1024,512]{1,0:T(8,128)(2,1)}, u32[]{:S(2)}) copy-start(bf16[1024,512]{1,0:T(8,128)(2,1)} %refs_1_.1) | copy-start | bytes 3145732
  27.9 6.5 %collective-permute-start.12 = (bf16[128,512]{1,0:T(8,128)(2,1)S(1)}, bf16[128,512]{1,0:T(8,128)(2,1)S(1)}, u32[]{:S(2)}, u32[]{:S(2)}) collective-permute-start(bf16[128,512]{1,0:T(8,128)(2,1)S(1)} %get-tuple-element.69), channel_id=1, source_target_pairs={{0,2},{1,3},{2,0},{3,1},{4,6},{5,7},{6,4},{7,5},{8,10},{9,11},{10,... | collective-permute-start | bytes 393224 | tf_op jit(solution)/shard_map/ppermute | solution.py:288
